TPU v7x, 128 devices: a whole 4x4x4 slice. The times are simulated.
128 devices in a mesh: ka: 32 (over x, z, core), ga: 4 (over y).
Axes of the slice: x: 4, y: 4, z: 4, core: 2. Of those that a mesh axis runs over, the one named last changes fastest.
Arguments:
- delta_rho: float32 [2048, 128], P('ka'), may hold values from -1.8 to 1.8
- bloch_blocks: float32 [2048, 2, 8, 6000], P('ka', None, None, 'ga'), may hold values from -1.5 to 1.5
- coulomb: float32 [6000], P('ga'), may hold values from 0.1 to 1
- energies: float32 [2048, 8], P('ka'), may hold values from -4 to 4
- dipole: float32 [2048, 128], P('ka'), may hold values from -3 to 3
- pair_count: int32 [256], replicated, may hold values from 1 to 8, as said below
- pair_target: int32 [256, 8], replicated, may hold values from 0 to 255, as said below
- kernel: float32 [256, 512], replicated, may hold values from -1 to 1
Outputs:
- delta_out: float32 [2048, 128], P('ka')
Inputs may be any that keep to these rules, and one draw needn't show every extreme that they name: `pair_count`: the blocks of one device (aligned runs of 8 blocks) always include one with all 8 entries live. `pair_target`: a k-block index; only the first pair_count[b] entries of row b are live. Among the live entries of the 8 blocks of one device, at most 2 have targets within the 8 blocks of any one device; in every draw some device receives exactly 2 live entries from every device.
All inputs are finite; a program needn't handle non-finite values.
Results may differ from a plain program's by a relative error of at most 0.00023.
Values sent between devices are 32-bit elements; how exact they have to be, the bound alone decides.
A program may use at most 64 MiB of HBM per device.

v0:
```python
import math

import jax
import jax.numpy as jnp
from jax import lax
from jax.sharding import PartitionSpec as P

NB = 8
KB = 8
MAXP = 8
STEPS = 3
NBLK = 8


time_step = 0.1
pulse_amp = 3.0
pulse_center = 0.15
pulse_width = 0.2
pulse_freq = 2.0
highest = lax.Precision.HIGHEST


def pulse_field(moment):
    return (
        pulse_amp
        * math.exp(-(((moment - pulse_center) / pulse_width) ** 2))
        * math.cos(pulse_freq * moment)
    )


def split_parts(flat_rows):
    pieces = flat_rows.reshape(flat_rows.shape[0], 2, NB, NB)
    return (pieces[:, 0], pieces[:, 1])


def join_parts(real_part, imag_part):
    return jnp.stack([real_part, imag_part], axis=1).reshape(real_part.shape[0], 2 * NB * NB)


def hermitian(flat_rows):
    real_part, imag_part = split_parts(flat_rows)
    return join_parts(
        0.5 * (real_part + jnp.swapaxes(real_part, 1, 2)),
        0.5 * (imag_part - jnp.swapaxes(imag_part, 1, 2)),
    )


def band_tables():
    flat_index = jnp.arange(2 * NB * NB)
    channel = flat_index // (NB * NB)
    row_band = flat_index // NB % NB
    col_band = flat_index % NB
    on_diag = (channel == 0) & (row_band == col_band)
    ground = (on_diag & (row_band < NB // 2)).astype(jnp.float32)
    diag_table = (on_diag[None, :] & (row_band[None, :] == jnp.arange(NB)[:, None])).astype(
        jnp.float32
    )
    return (ground, diag_table)


def mat_prod(left_mat, right_mat):
    return jnp.einsum("kij,kjl->kil", left_mat, right_mat, precision=highest)


def change_of(hamilton, density_rows):
    ham_re, ham_im = split_parts(hamilton)
    rho_re, rho_im = split_parts(density_rows)
    comm_re = (
        mat_prod(ham_re, rho_re)
        - mat_prod(ham_im, rho_im)
        - mat_prod(rho_re, ham_re)
        + mat_prod(rho_im, ham_im)
    )
    comm_im = (
        mat_prod(ham_re, rho_im)
        + mat_prod(ham_im, rho_re)
        - mat_prod(rho_re, ham_im)
        - mat_prod(rho_im, ham_re)
    )
    return join_parts(comm_im, -comm_re)


def coupling_matrix(delta_rows):
    real_part, imag_part = split_parts(delta_rows)
    upper_rows = jnp.concatenate([real_part, -imag_part], axis=2)
    lower_rows = jnp.concatenate([imag_part, real_part], axis=2)
    return jnp.concatenate([upper_rows, lower_rows], axis=1)


def gram_to_rows(gram_sums):
    ham_re = gram_sums[:, :NB, :NB] + gram_sums[:, NB:, NB:]
    ham_im = gram_sums[:, :NB, NB:] - gram_sums[:, NB:, :NB]
    return join_parts(ham_re, ham_im)


def hartree_local(delta_rows, orbitals, coulomb, total_k):
    applied = jnp.einsum("kab,kbg->kag", coupling_matrix(delta_rows), orbitals, precision=highest)
    own_density = jnp.sum(orbitals * applied, axis=(0, 1))
    density = lax.psum(own_density, "ka")
    potential = coulomb * density / total_k
    gram_sums = jnp.einsum("kag,kbg->kab", orbitals * potential, orbitals, precision=highest)
    return gram_to_rows(gram_sums)


def gathered_products(delta_rows, pair_count, pair_target, kernel):
    my_rank = lax.axis_index("ka")
    slot_share = MAXP // lax.axis_size("ga")
    first_slot = lax.axis_index("ga") * slot_share
    width_row = KB * 2 * NB * NB
    source_rows = lax.all_gather(delta_rows.reshape(NBLK, width_row), "ka", axis=0, tiled=True)
    source_count = source_rows.shape[0]
    target_rows = pair_target
    target_rows = lax.dynamic_slice_in_dim(target_rows, first_slot, slot_share, 1)
    kernel_rows = kernel
    kernel_rows = lax.dynamic_slice_in_dim(
        kernel_rows, first_slot * KB * KB, slot_share * KB * KB, 1
    )
    kernel_rows = kernel_rows.reshape(source_count, slot_share, KB, KB)
    slot_number = first_slot + jnp.arange(slot_share)
    wanted = (slot_number[None, :] < pair_count[:, None]) & (target_rows // NBLK == my_rank)
    one_hot = (
        wanted[:, :, None] & ((target_rows % NBLK)[:, :, None] == jnp.arange(NBLK)[None, None, :])
    ).astype(jnp.float32)
    products = jnp.einsum(
        "bpkl,blc->bpkc",
        kernel_rows,
        source_rows.reshape(source_count, KB, 2 * NB * NB),
        precision=highest,
    )
    folded = jnp.einsum("bpq,bpkc->qkc", one_hot, products, precision=highest)
    return -folded.reshape(NBLK * KB, 2 * NB * NB)


def local(delta_rho, bloch_blocks, coulomb, energies, dipole, pair_count, pair_target, kernel):
    orbitals = bloch_blocks.reshape(bloch_blocks.shape[0], 2 * NB, bloch_blocks.shape[3])
    ground, diag_table = band_tables()
    band_diag = jnp.dot(energies, diag_table, precision=highest)
    dipole_h = hermitian(dipole)
    total_k = delta_rho.shape[0] * lax.axis_size("ka")

    def hamiltonian(delta_rows, moment):
        hartree_part = hartree_local(delta_rows, orbitals, coulomb, total_k)
        local_terms = hartree_part + gathered_products(delta_rows, pair_count, pair_target, kernel)
        summed = lax.psum(local_terms, "ga")
        return band_diag + pulse_field(moment) * dipole_h + summed

    current = hermitian(delta_rho)
    for step_number in range(STEPS):
        moment = step_number * time_step
        half_step = current + 0.5 * time_step * change_of(
            hamiltonian(current, moment), current + ground
        )
        current = current + time_step * change_of(
            hamiltonian(half_step, moment + 0.5 * time_step), half_step + ground
        )
    return current


def solution(mesh):
    in_specs = (
        P("ka", None),
        P("ka", None, None, "ga"),
        P("ga"),
        P("ka", None),
        P("ka", None),
        P(),
        P(),
        P(),
    )
    out_specs = P("ka", None)
    return jax.shard_map(local, mesh=mesh, in_specs=in_specs, out_specs=out_specs, check_vma=False)
```

profile of v0, /device:TPU:1, one launch (start us, length us, event | category | flops | bytes accessed | tf_op | source)
XLA Modules:
  0.0 768.7 jit_solution(3680785757371075352)
XLA Ops:
  9.3 10.2 %fusion.30 = f32[1500]{0:T(1024)S(1)} fusion(f32[64,2,8,1500]{3,2,1,0:T(8,128)} %param.9, f32[64,16,16]{2,1,0:T(8,128)S(1)} %copy.249), kind=kOutput, calls=%fused_computation.36 | convolution fusion | flops 297982496 | bytes 6215536 | tf_op jit(solution)/shard_map/kab,kbg->kag/dot_general | solution.py:97
  19.6 66.1 %psum.84 = f32[1500]{0:T(1024)S(1)} all-reduce(f32[1500]{0:T(1024)S(1)} %fusion.30), channel_id=1, replica_groups=mesh['ka'=32,'ga'=4] {'ka'}, use_global_device_ids=true, to_apply=%region_1.2 | all-reduce | flops 1500 | bytes 12000 | tf_op jit(solution)/shard_map/psum | solution.py:99
  85.8 13.5 %fusion.10 = f32[64,16,16]{2,1,0:T(8,128)S(1)} fusion(f32[64,2,8,1500]{3,2,1,0:T(8,128)} %param.9, f32[1500]{0:T(1024)S(1)} %multiply_multiply_fusion.5), kind=kOutput, calls=%fused_computation.10 | convolution fusion | flops 296448000 | bytes 6215536 | tf_op jit(solution)/shard_map/kag,kbg->kab/dot_general | solution.py:101
  106.6 1.4 copy.380
  108.0 2.0 fusion.130
  110.0 1.3 fusion.87
  111.3 14.0 %psum.85 = f32[64,128]{1,0:T(8,128)S(1)} all-reduce(f32[64,128]{1,0:T(8,128)S(1)} %bitcast_add_fusion.7), channel_id=1, replica_groups=mesh['ka'=32,'ga'=4] {'ga'}, use_global_device_ids=true, to_apply=%region_2.3 | all-reduce | flops 8192 | bytes 65536 | tf_op jit(solution)/shard_map/psum | solution.py:144
  127.9 1.3 fusion.199
  131.2 1.6 convolution_subtract_fusion.21
  133.4 1.5 fusion.82
  134.9 1.6 convolution_add_fusion.11
  136.5 1.5 convolution_subtract_fusion.23
  143.3 10.2 %fusion.31 = f32[1500]{0:T(1024)S(1)} fusion(f32[64,2,8,1500]{3,2,1,0:T(8,128)} %param.9, f32[64,16,16]{2,1,0:T(8,128)S(1)} %copy.267), kind=kOutput, calls=%fused_computation.37 | convolution fusion | flops 297982496 | bytes 6215536 | tf_op jit(solution)/shard_map/kab,kbg->kag/dot_general | solution.py:97
  153.5 72.6 %psum.86 = f32[1500]{0:T(1024)S(1)} all-reduce(f32[1500]{0:T(1024)S(1)} %fusion.31), channel_id=1, replica_groups=mesh['ka'=32,'ga'=4] {'ka'}, use_global_device_ids=true, to_apply=%region_4.5 | all-reduce | flops 1500 | bytes 12000 | tf_op jit(solution)/shard_map/psum | solution.py:99
  226.1 13.5 %fusion.8 = f32[64,16,16]{2,1,0:T(8,128)S(1)} fusion(f32[64,2,8,1500]{3,2,1,0:T(8,128)} %param.9, f32[1500]{0:T(1024)S(1)} %multiply_multiply_fusion.4), kind=kOutput, calls=%fused_computation.8 | convolution fusion | flops 296448000 | bytes 6215536 | tf_op jit(solution)/shard_map/kag,kbg->kab/dot_general | solution.py:101
  240.2 1.4 copy.381
  241.7 2.0 fusion.128
  243.6 1.3 fusion.93
  245.0 11.5 %psum.87 = f32[64,128]{1,0:T(8,128)S(1)} all-reduce(f32[64,128]{1,0:T(8,128)S(1)} %bitcast_add_fusion.6), channel_id=1, replica_groups=mesh['ka'=32,'ga'=4] {'ga'}, use_global_device_ids=true, to_apply=%region_5.6 | all-reduce | flops 8192 | bytes 65536 | tf_op jit(solution)/shard_map/psum | solution.py:144
  257.3 1.3 fusion.192
  260.4 1.5 convolution_add_fusion.9
  265.1 1.3 mul.268
  270.3 8.8 %fusion.32 = f32[1500]{0:T(1024)S(1)} fusion(f32[64,2,8,1500]{3,2,1,0:T(8,128)} %param.9, f32[64,16,16]{2,1,0:T(8,128)} %copy.285), kind=kOutput, calls=%fused_computation.38 | convolution fusion | flops 297982496 | bytes 6215536 | tf_op jit(solution)/shard_map/kab,kbg->kag/dot_general | solution.py:97
  279.1 67.1 %psum.88 = f32[1500]{0:T(1024)S(1)} all-reduce(f32[1500]{0:T(1024)S(1)} %fusion.32), channel_id=1, replica_groups=mesh['ka'=32,'ga'=4] {'ka'}, use_global_device_ids=true, to_apply=%region_7.8 | all-reduce | flops 1500 | bytes 12000 | tf_op jit(solution)/shard_map/psum | solution.py:99
  346.2 13.5 %fusion.6 = f32[64,16,16]{2,1,0:T(8,128)S(1)} fusion(f32[64,2,8,1500]{3,2,1,0:T(8,128)} %param.9, f32[1500]{0:T(1024)S(1)} %multiply_multiply_fusion.3), kind=kOutput, calls=%fused_computation.6 | convolution fusion | flops 296448000 | bytes 6215536 | tf_op jit(solution)/shard_map/kag,kbg->kab/dot_general | solution.py:101
  361.9 1.4 copy.382
  363.3 2.0 fusion.126
  365.3 1.3 fusion.99
  366.6 12.9 %psum.89 = f32[64,128]{1,0:T(8,128)S(1)} all-reduce(f32[64,128]{1,0:T(8,128)S(1)} %bitcast_add_fusion.5), channel_id=1, replica_groups=mesh['ka'=32,'ga'=4] {'ga'}, use_global_device_ids=true, to_apply=%region_8.9 | all-reduce | flops 8192 | bytes 65536 | tf_op jit(solution)/shard_map/psum | solution.py:144
  383.2 1.6 convolution_subtract_fusion.13
  385.3 1.5 fusion.76
  386.9 1.6 convolution_add_fusion.7
  388.5 1.5 convolution_subtract_fusion.15
  395.2 10.2 %fusion.33 = f32[1500]{0:T(1024)S(1)} fusion(f32[64,2,8,1500]{3,2,1,0:T(8,128)} %param.9, f32[64,16,16]{2,1,0:T(8,128)S(1)} %copy.300), kind=kOutput, calls=%fused_computation.39 | convolution fusion | flops 297982496 | bytes 6215536 | tf_op jit(solution)/shard_map/kab,kbg->kag/dot_general | solution.py:97
  405.5 68.2 %psum.90 = f32[1500]{0:T(1024)S(1)} all-reduce(f32[1500]{0:T(1024)S(1)} %fusion.33), channel_id=1, replica_groups=mesh['ka'=32,'ga'=4] {'ka'}, use_global_device_ids=true, to_apply=%region_10.11 | all-reduce | flops 1500 | bytes 12000 | tf_op jit(solution)/shard_map/psum | solution.py:99
  473.7 13.5 %fusion.4 = f32[64,16,16]{2,1,0:T(8,128)S(1)} fusion(f32[64,2,8,1500]{3,2,1,0:T(8,128)} %param.9, f32[1500]{0:T(1024)S(1)} %multiply_multiply_fusion.2), kind=kOutput, calls=%fused_computation.4 | convolution fusion | flops 296448000 | bytes 6215536 | tf_op jit(solution)/shard_map/kag,kbg->kab/dot_general | solution.py:101
  487.8 1.4 copy.383
  489.2 2.0 fusion.124
  491.2 1.3 fusion.105
  492.5 11.3 %psum.91 = f32[64,128]{1,0:T(8,128)S(1)} all-reduce(f32[64,128]{1,0:T(8,128)S(1)} %bitcast_add_fusion.4), channel_id=1, replica_groups=mesh['ka'=32,'ga'=4] {'ga'}, use_global_device_ids=true, to_apply=%region_11.12 | all-reduce | flops 8192 | bytes 65536 | tf_op jit(solution)/shard_map/psum | solution.py:144
  504.7 1.3 fusion.172
  507.9 1.5 convolution_add_fusion.5
  512.5 1.3 mul.286
  517.7 8.8 %fusion.35 = f32[1500]{0:T(1024)S(1)} fusion(f32[64,2,8,1500]{3,2,1,0:T(8,128)} %param.9, f32[64,16,16]{2,1,0:T(8,128)} %copy.317), kind=kOutput, calls=%fused_computation.41 | convolution fusion | flops 297982496 | bytes 6215536 | tf_op jit(solution)/shard_map/kab,kbg->kag/dot_general | solution.py:97
  526.5 67.1 %psum.92 = f32[1500]{0:T(1024)S(1)} all-reduce(f32[1500]{0:T(1024)S(1)} %fusion.35), channel_id=1, replica_groups=mesh['ka'=32,'ga'=4] {'ka'}, use_global_device_ids=true, to_apply=%region_13.14 | all-reduce | flops 1500 | bytes 12000 | tf_op jit(solution)/shard_map/psum | solution.py:99
  593.6 13.5 %fusion.2 = f32[64,16,16]{2,1,0:T(8,128)S(1)} fusion(f32[64,2,8,1500]{3,2,1,0:T(8,128)} %param.9, f32[1500]{0:T(1024)S(1)} %multiply_multiply_fusion.1), kind=kOutput, calls=%fused_computation.2 | convolution fusion | flops 296448000 | bytes 6215536 | tf_op jit(solution)/shard_map/kag,kbg->kab/dot_general | solution.py:101
  609.3 1.4 copy.384
  610.8 2.0 fusion.122
  612.8 1.3 fusion.111
  614.1 12.9 %psum.93 = f32[64,128]{1,0:T(8,128)S(1)} all-reduce(f32[64,128]{1,0:T(8,128)S(1)} %bitcast_add_fusion.3), channel_id=1, replica_groups=mesh['ka'=32,'ga'=4] {'ga'}, use_global_device_ids=true, to_apply=%region_14.15 | all-reduce | flops 8192 | bytes 65536 | tf_op jit(solution)/shard_map/psum | solution.py:144
  627.3 1.3 fusion.159
  630.6 1.6 convolution_subtract_fusion.5
  632.8 1.5 fusion.70
  634.3 1.6 convolution_add_fusion.3
  635.9 1.5 convolution_subtract_fusion.7
  639.7 1.3 mul.292
  641.7 1.8 slice_bitcast_fusion.2
  646.9 8.8 %fusion.34 = f32[1500]{0:T(1024)S(1)} fusion(f32[64,2,8,1500]{3,2,1,0:T(8,128)} %param.9, f32[64,16,16]{2,1,0:T(8,128)} %copy.332), kind=kOutput, calls=%fused_computation.40 | convolution fusion | flops 297982496 | bytes 6215536 | tf_op jit(solution)/shard_map/kab,kbg->kag/dot_general | solution.py:97
  655.7 67.9 %psum.94 = f32[1500]{0:T(1024)S(1)} all-reduce(f32[1500]{0:T(1024)S(1)} %fusion.34), channel_id=1, replica_groups=mesh['ka'=32,'ga'=4] {'ka'}, use_global_device_ids=true, to_apply=%region_16.17 | all-reduce | flops 1500 | bytes 12000 | tf_op jit(solution)/shard_map/psum | solution.py:99
  723.5 13.5 %fusion = f32[64,16,16]{2,1,0:T(8,128)S(1)} fusion(f32[64,2,8,1500]{3,2,1,0:T(8,128)} %param.9, f32[1500]{0:T(1024)S(1)} %multiply_multiply_fusion), kind=kOutput, calls=%fused_computation | convolution fusion | flops 296448000 | bytes 6215536 | tf_op jit(solution)/shard_map/kag,kbg->kab/dot_general | solution.py:101
  739.3 1.4 copy.385
  740.7 2.0 fusion.120
  742.7 1.3 fusion.117
  744.0 11.1 %psum.95 = f32[64,128]{1,0:T(8,128)S(1)} all-reduce(f32[64,128]{1,0:T(8,128)S(1)} %bitcast_add_fusion.2), channel_id=1, replica_groups=mesh['ka'=32,'ga'=4] {'ga'}, use_global_device_ids=true, to_apply=%region_17.18 | all-reduce | flops 8192 | bytes 65536 | tf_op jit(solution)/shard_map/psum | solution.py:144
  (259 shorter events, 72.4 us)
Async XLA Ops:
  6.5 93.3 %copy-start = (f32[256,512]{1,0:T(8,128)S(1)}, f32[256,512]{1,0:T(8,128)}, u32[]{:S(2)}) copy-start(f32[256,512]{1,0:T(8,128)} %param.15) | copy-start | bytes 1572868
  6.5 79.2 %copy-start.6 = (f32[1500]{0:T(1024)S(1)}, f32[1500]{0:T(1024)}, u32[]{:S(2)}) copy-start(f32[1500]{0:T(1024)} %param.10) | copy-start | bytes 18004
  6.5 100.0 %all-gather.7.cloned.1.call-start = ((), (), s32[]{:S(2)}) async-start(), calls=%async_computation | async-start | bytes 1081344 | tf_op jit(solution)/shard_map/all_gather | solution.py:110
  8.7 231.5 %all-gather.9.cloned.1.call-start = ((), (), s32[]{:S(2)}) async-start(), calls=%async_computation.1 | async-start | bytes 1081344 | tf_op jit(solution)/shard_map/all_gather | solution.py:110
  9.0 129.6 %copy-start.3 = (f32[64,2,8,8]{3,2,0,1:T(8,128)}, f32[64,2,8,8]{3,2,0,1:T(8,128)S(1)}, u32[]{:S(2)}) copy-start(f32[64,2,8,8]{3,2,0,1:T(8,128)S(1)} %copy.278) | copy-start | bytes 98308
  85.7 15.5 %copy-start.25 = (f32[64,128]{1,0:T(8,128)S(1)}, f32[64,128]{1,0:T(8,128)}, u32[]{:S(2)}) copy-start(f32[64,128]{1,0:T(8,128)} %param.12) | copy-start | bytes 98308
  102.2 23.1 %copy-start.12 = (f32[64,128]{1,0:T(8,128)S(1)}, f32[64,128]{1,0:T(8,128)}, u32[]{:S(2)}) copy-start(f32[64,128]{1,0:T(8,128)} %copy.248) | copy-start | bytes 98308
  105.7 4.3 copy-start.13
  106.5 3.5 copy-start.19
  127.0 12.9 %copy-start.4 = (f32[8,1024]{1,0:T(8,128)S(1)}, f32[8,1024]{1,0:T(8,128)}, u32[]{:S(2)}) copy-start(f32[8,1024]{1,0:T(8,128)} %reshape_reshape.3) | copy-start | bytes 98308
  140.5 221.4 %all-gather.11.cloned.1.call-start = ((), (), s32[]{:S(2)}) async-start(), calls=%async_computation.2 | async-start | bytes 1081344 | tf_op jit(solution)/shard_map/all_gather | solution.py:110
  239.6 4.0 copy-start.14
  239.6 4.0 copy-start.20
  264.2 126.3 %copy-start.2 = (f32[64,2,8,8]{3,2,0,1:T(8,128)}, f32[64,2,8,8]{3,2,0,1:T(8,128)S(1)}, u32[]{:S(2)}) copy-start(f32[64,2,8,8]{3,2,0,1:T(8,128)S(1)} %get-tuple-element.12) | copy-start | bytes 98308
  267.1 220.7 %all-gather.13.cloned.1.call-start = ((), (), s32[]{:S(2)}) async-start(), calls=%async_computation.3 | async-start | bytes 1081344 | tf_op jit(solution)/shard_map/all_gather | solution.py:110
  359.7 19.9 %copy-start.11 = (f32[64,128]{1,0:T(8,128)S(1)}, f32[64,128]{1,0:T(8,128)}, u32[]{:S(2)}) copy-start(f32[64,128]{1,0:T(8,128)} %copy.280) | copy-start | bytes 98308
  361.7 3.5 copy-start.15
  361.7 3.5 copy-start.21
  379.7 12.1 %copy-start.5 = (f32[8,1024]{1,0:T(8,128)S(1)}, f32[8,1024]{1,0:T(8,128)}, u32[]{:S(2)}) copy-start(f32[8,1024]{1,0:T(8,128)} %add.419) | copy-start | bytes 98308
  392.4 216.9 %all-gather.15.cloned.1.call-start = ((), (), s32[]{:S(2)}) async-start(), calls=%async_computation.4 | async-start | bytes 1081344 | tf_op jit(solution)/shard_map/all_gather | solution.py:110
  487.2 4.0 copy-start.16
  487.2 4.0 copy-start.22
  487.2 16.7 %copy-start.10 = (f32[64,128]{1,0:T(8,128)S(1)}, f32[64,128]{1,0:T(8,128)}, u32[]{:S(2)}) copy-start(f32[64,128]{1,0:T(8,128)} %copy.279) | copy-start | bytes 98308
  514.4 224.8 %all-gather.17.cloned.1.call-start = ((), (), s32[]{:S(2)}) async-start(), calls=%async_computation.5 | async-start | bytes 1081344 | tf_op jit(solution)/shard_map/all_gather | solution.py:110
  607.1 19.9 %copy-start.9 = (f32[64,128]{1,0:T(8,128)S(1)}, f32[64,128]{1,0:T(8,128)}, u32[]{:S(2)}) copy-start(f32[64,128]{1,0:T(8,128)} %copy.312) | copy-start | bytes 98308
  609.2 3.5 copy-start.17
  609.2 3.5 copy-start.23
  627.1 13.9 %copy-start.7 = (f32[8,1024]{1,0:T(8,128)S(1)}, f32[8,1024]{1,0:T(8,128)}, u32[]{:S(2)}) copy-start(f32[8,1024]{1,0:T(8,128)} %add.437) | copy-start | bytes 98308
  737.0 5.6 copy-start.18
  737.0 5.6 copy-start.24
  737.0 18.1 %copy-start.8 = (f32[64,128]{1,0:T(8,128)S(1)}, f32[64,128]{1,0:T(8,128)}, u32[]{:S(2)}) copy-start(f32[64,128]{1,0:T(8,128)} %copy.311) | copy-start | bytes 98308
  742.7 18.9 %copy-start.1 = (f32[256,512]{1,0:T(8,128)S(1)}, f32[256,512]{1,0:T(8,128)}, u32[]{:S(2)}) copy-start(f32[256,512]{1,0:T(8,128)} %param.15) | copy-start | bytes 1572868
Sparse Core Ops, SparseCore 0:
  9.6 46.5 all-gather.6
  140.6 46.1 all-gather.8
  267.2 41.7 all-gather.10
  392.5 41.9 all-gather.12
  514.6 41.7 all-gather.14
  641.8 41.7 all-gather.16
where the time goes:
time: 777 us; the launch traced here: 769 us
  blocking collectives  483 us (62%)
  matrix products  205 us (26%)
  local copies, waits for them, and re-layouts  49 us (6%)
  other arithmetic  16.6 us (2%)
  between operations  15 us (2%)
    psum x6, blocking collectives, hartree_local(): density = lax.psum(own_density, 'ka')  409 us
    dot_general x6, matrix products, hartree_local(): jnp.einsum('kag,kbg->kab', orbitals * potential, orbitals, precision=high...  81 us
    psum x6, blocking collectives, hamiltonian(): summed = lax.psum(local_terms, 'ga')  73.6 us
    dot_general x6, matrix products, hartree_local(): jnp.einsum('kab,kbg->kag', coupling_matrix(delta_rows), orbitals, precisi...  57.1 us
    dot_general x48, matrix products, mat_prod(): return jnp.einsum('kij,kjl->kil', left_mat, right_mat, precision=highest)  46.2 us
  transfers between devices with their start and end apart: 6, of which 0 were waited for; matrix products, arithmetic and copies ran while one was open for 22% of the time, Pallas kernels for 0%

commit v1 on v0

v1 whole, which is shorter than its diff:
```python
import functools
import math

import jax
import jax.numpy as jnp
import numpy as np
from jax import lax
from jax.experimental import pallas as pl
from jax.experimental.pallas import tpu as pltpu
from jax.sharding import PartitionSpec as P

NB = 8
KB = 8
MAXP = 8
STEPS = 3
NBLK = 8
NK = 64
NG = 1500
TILES = 12
WIDE = TILES * 128
CHIPS = 16
SIDE = 4
CHUNKS = 8

time_step = 0.1
pulse_amp = 3.0
pulse_center = 0.15
pulse_width = 0.2
pulse_freq = 2.0
highest = lax.Precision.HIGHEST
MESH = pl.DeviceIdType.MESH
f32 = jnp.float32

PLANE = [(a, b) for a in range(SIDE) for b in range(SIDE) if (a, b) != (0, 0)]


def pulse_field(moment):
    return (
        pulse_amp
        * math.exp(-(((moment - pulse_center) / pulse_width) ** 2))
        * math.cos(pulse_freq * moment)
    )


def component_tables():
    into = np.zeros((64, 128), np.float32)
    back = np.zeros((64, 128), np.float32)

    def real_entry(row, i, j):
        into[row, i * 8 + j] += 0.5
        into[row, j * 8 + i] += 0.5
        back[row, i * 8 + j] = 1.0
        back[row, j * 8 + i] = 1.0

    def imag_entry(row, i, j):
        into[row, 64 + i * 8 + j] += 0.5
        into[row, 64 + j * 8 + i] -= 0.5
        back[row, 64 + i * 8 + j] = 1.0
        back[row, 64 + j * 8 + i] = -1.0

    for i in range(8):
        real_entry(i, i, i)
        if i < 4:
            real_entry(8 + i, i, i + 4)
        else:
            imag_entry(8 + i, i, i - 4)
        for v in (1, 2, 3):
            real_entry(16 * v + i, i, (i + v) % 8)
            imag_entry(16 * v + 8 + i, i, (i + v) % 8)
    return into, back


def dot(a, b, lhs_dim, rhs_dim, precision=highest):
    return lax.dot_general(
        a, b, (((lhs_dim,), (rhs_dim,)), ((), ())), precision=precision, preferred_element_type=f32
    )


def iota(shape, axis):
    return lax.broadcasted_iota(jnp.int32, shape, axis)


def merge(a, b, bit):
    low = (iota((8, 128), 1) & (1 << bit)) == 0
    return jnp.where(low, a, b) + pltpu.roll(jnp.where(low, b, a), 1 << bit, 1)


def merge_all(values, bit):
    while len(values) > 1:
        values = [merge(a, b, bit) for a, b in zip(values[0::2], values[1::2])]
        bit += 1
    return values[0]


def rolled(value, up):
    up = up % 8
    return value if up == 0 else pltpu.roll(value, 8 - up, 0)


def swap(value):
    return pltpu.roll(value, 64, 1)


def offsets_of(packed):
    left = iota((8, 128), 1) < 64
    top = iota((8, 128), 0) < 4
    mixed_right = packed[0]
    mixed_left = swap(packed[0])
    zeroth = jnp.where(left, packed[0], 0.0)
    fourth = jnp.where(
        left,
        jnp.where(top, mixed_left, rolled(mixed_left, 4)),
        jnp.where(top, -rolled(mixed_right, 4), mixed_right),
    )
    diags = [zeroth, packed[1], packed[2], packed[3], fourth]
    for offset in (5, 6, 7):
        turned = rolled(diags[8 - offset], offset)
        diags.append(jnp.where(left, turned, -turned))
    return diags


def change_of(hamilton, state):
    left = iota((8, 128), 1) < 64
    top = iota((8, 128), 0) < 4
    ham = offsets_of(hamilton)
    rho = offsets_of(state)
    ham_swapped = [swap(h) for h in ham]
    ham_re = [jnp.where(left, h, s) for h, s in zip(ham, ham_swapped)]
    ham_im = [jnp.where(left, s, h) for h, s in zip(ham, ham_swapped)]
    products = []
    turned = [[rolled(rho[f], e) for e in range(8)] for f in range(8)]
    for d in range(8):
        from_re = None
        from_im = None
        for e in range(8):
            factor = turned[(d - e) % 8][e]
            term_re = ham_re[e] * factor
            from_re = term_re if e == 0 else from_re + term_re
            if e > 0:
                term_im = ham_im[e] * factor
                from_im = term_im if from_im is None else from_im + term_im
        crossed = swap(from_im)
        products.append(from_re + jnp.where(left, -crossed, crossed))
    changes = []
    for d in range(5):
        other = rolled(products[(8 - d) % 8], d)
        diff = products[d] - jnp.where(left, other, -other)
        crossed = swap(diff)
        changes.append(jnp.where(left, crossed, -crossed))
    mixed = jnp.where(top, swap(changes[4]), changes[4])
    return [jnp.where(left, changes[0], mixed)] + changes[1:4]


def kernel(
    rho_hbm, bloch_hbm, coulomb_hbm, energies_hbm, dipole_hbm, count_smem, target_hbm, kernel_hbm, into_hbm, back_hbm,
    out_ref,
    rho_buf, bands, coulomb_buf, energies_buf, dipole_buf, target_buf, kernel_buf, into_buf, back_buf,
    pairs, tail, partial, own_terms, couple, coulomb_rows,
    rho_send, rho_recv, core_send, core_recv, plane_send, plane_recv, sig_send, sig_recv, ham_recv,
    load_sem, band_sem, send_sem, recv_sem,
):
    ka = lax.axis_index("ka")
    ga = lax.axis_index("ga")
    core = lax.rem(ka, 2)
    chip = ka // 2
    chip_x = chip // SIDE
    chip_z = lax.rem(chip, SIDE)

    partner = (chip * 2 + (1 - core), ga)
    plane_chips = [
        lax.rem(chip_x + a, SIDE) * SIDE + lax.rem(chip_z + b, SIDE) for a, b in PLANE
    ]
    plane_ids = [(c * 2 + core, ga) for c in plane_chips]
    line_ids = [(ka, lax.rem(ga + d, SIDE)) for d in (1, 2, 3)]

    barrier = pltpu.get_barrier_semaphore()
    everyone = [partner] + plane_ids + line_ids
    for device in everyone:
        pl.semaphore_signal(barrier, inc=1, device_id=device, device_id_type=MESH)

    step_k = NK // CHUNKS
    band_loads = [
        pltpu.make_async_copy(
            bloch_hbm.at[pl.ds(n * step_k, step_k)],
            bands.at[pl.ds(n * step_k, step_k)],
            band_sem.at[n],
        )
        for n in range(CHUNKS)
    ]
    first_block = pl.multiple_of(chip * 16, 16)
    loads = [
        pltpu.make_async_copy(src, dst, load_sem.at[n])
        for n, (src, dst) in enumerate(
            [
                (rho_hbm, rho_buf),
                (into_hbm, into_buf),
                (dipole_hbm, dipole_buf),
                (energies_hbm, energies_buf),
                (coulomb_hbm, coulomb_buf),
                (target_hbm.at[pl.ds(first_block, 16)], target_buf),
                (kernel_hbm.at[pl.ds(first_block, 16)], kernel_buf),
                (back_hbm, back_buf),
            ]
        )
    ]
    for copy in loads:
        copy.start()
    for copy in band_loads:
        copy.start()

    lane = iota((8, 128), 1)
    row = iota((8, 128), 0)
    left = lane < 64
    top = row < 4

    tail[...] = jnp.zeros((NK, 2, 8, 128), f32)
    coulomb_rows[...] = jnp.zeros((16, 128), f32)

    for copy in loads:
        copy.wait()

    def packed_rows(rows):
        comps = dot(into_buf[...], jnp.concatenate([rows, rows], axis=0), 1, 1)
        return [
            jnp.where(left, comps[16 * v : 16 * v + 8], comps[16 * v + 8 : 16 * v + 16])
            for v in range(4)
        ]

    start = packed_rows(rho_buf[...])
    dipole_h = packed_rows(dipole_buf[...])
    unit = (iota((8, 8), 0) == iota((8, 8), 1)).astype(f32)
    level = dot(unit, jnp.concatenate([energies_buf[...]] * 2, axis=0), 1, 1)
    band_diag = jnp.where(left, level, 0.0)
    ground = jnp.where(left & top, 1.0, 0.0)

    for j in range(TILES):
        width = min(128, NG - j * 128)
        coulomb_rows[j : j + 1, 0:width] = coulomb_buf[0:1, j * 128 : j * 128 + width] * (1.0 / 2048.0)

    spread = (iota((8, 128), 1) // 16 == iota((8, 128), 0)).astype(f32)
    wide_target = dot(target_buf[...].astype(f32), spread, 1, 0)
    on_row = lax.rem(iota((16, 128), 1), 16) == iota((16, 128), 0)
    target_line = jnp.sum(jnp.where(on_row, wide_target, 0.0), axis=0, keepdims=True)
    lane_line = iota((1, 128), 1)
    count_line = jnp.zeros((1, 128), jnp.int32)
    for b in range(16):
        count_line = jnp.where(lax.rem(lane_line, 16) == b, count_smem[chip * 16 + b], count_line)
    live = lane_line // 16 < count_line
    wide_row = iota((128, 128), 0)
    wide_lane = iota((128, 128), 1)
    block_of_row = ((wide_row // 8) * 2 + core) * 8 + lax.rem(wide_row, 8)
    line = jnp.where(live, target_line, -1.0)
    hot = (line == block_of_row.astype(f32)).astype(f32)
    entry_rows = jnp.concatenate(
        [kernel_buf[:, p * 64 : (p + 1) * 64] for p in range(MAXP)], axis=0
    )
    for part in range(2):
        pick_row = iota((64, 128), 0)
        pick = (pick_row // 8 == 2 * ga + part) & (
            lax.rem(pick_row, 8) == lax.rem(iota((64, 128), 1), 8)
        )
        spread_rows = dot(entry_rows, pick.astype(f32), 1, 0)
        spread_rows = jnp.where(lax.rem(wide_row, 16) == wide_lane // 8, spread_rows, 0.0)
        couple[part] = -dot(hot, spread_rows, 1, 0)

    def build(k, _):
        last = (TILES - 1) * 128
        for part in range(2):
            tail[k, part, :, : NG - last] = bands[k, part, :, last:]
        for j in range(TILES):
            lanes = slice(j * 128, (j + 1) * 128)
            if j < TILES - 1:
                u, v = bands[k, 0, :, lanes], bands[k, 1, :, lanes]
            else:
                u, v = tail[k, 0], tail[k, 1]
            us = [u] + [rolled(u, d) for d in (1, 2, 3, 4)]
            vs = [v] + [rolled(v, d) for d in (1, 2, 3, 4)]
            values = [
                u * u + v * v,
                u * jnp.where(top, us[4], vs[4]) + v * jnp.where(top, vs[4], -us[4]),
            ]
            for d in (1, 2, 3):
                values += [u * us[d] + v * vs[d], u * vs[d] - v * us[d]]
            for t, value in enumerate(values):
                pairs[k * 8 + t, :, lanes] = value
        return 0

    for n, copy in enumerate(band_loads):
        copy.wait()
        lax.fori_loop(n * step_k, (n + 1) * step_k, build, 0)

    factors = [jnp.where(left, 1.0, jnp.where(top, 2.0, -2.0))] + [jnp.where(left, 2.0, -2.0)] * 3

    def density_of(state):
        weights = [f * s for f, s in zip(factors, state)]

        def add(step, sums):
            sums = list(sums)
            for r in range(2):
                k = step * 2 + r
                for half in range(2):
                    at = jnp.full((8, 128), half * 64 + k, jnp.int32)
                    for v in range(4):
                        weight = jnp.take_along_axis(weights[v], at, axis=1, mode="promise_in_bounds")
                        for j in range(TILES):
                            sums[j] = sums[j] + weight * pairs[k * 8 + 2 * v + half, :, j * 128 : (j + 1) * 128]
            return tuple(sums)

        zero = jnp.zeros((8, 128), f32)
        return lax.fori_loop(0, NK // 2, add, (zero,) * TILES)

    def gram_of(potential_rows):
        spread_v = [jnp.broadcast_to(potential_rows[j : j + 1], (8, 128)) for j in range(TILES)]

        def group(g, _):
            for t in range(8):
                sums = []
                for r in range(8):
                    k = g * 8 + r
                    total = None
                    for j in range(TILES):
                        term = spread_v[j] * pairs[k * 8 + t, :, j * 128 : (j + 1) * 128]
                        total = term if total is None else total + term
                    sums.append(total)
                partial[g * 8 + t] = merge_all(sums, 0)
            return 0

        lax.fori_loop(0, NK // 8, group, 0)
        packed = []
        for v in range(4):
            halves = [
                merge_all([partial[g * 8 + 2 * v + half] for g in range(8)], 3) for half in range(2)
            ]
            packed.append(merge(halves[0], halves[1], 6))
        return packed

    def remote(src, dst, send, recv, device):
        return pltpu.make_async_remote_copy(
            src_ref=src, dst_ref=dst, send_sem=send, recv_sem=recv, device_id=device, device_id_type=MESH
        )

    def wait_bytes(ref, sem):
        pltpu.make_async_copy(ref, ref, sem).wait()

    pl.semaphore_wait(barrier, len(everyone))

    def evaluate(e, carry):
        base, now = list(carry[:4]), list(carry[4:])
        par = lax.rem(e, 2)
        for v in range(4):
            rho_send[par, v] = now[v]
        to_partner = remote(
            rho_send.at[par], rho_recv.at[par], send_sem.at[0, par], recv_sem.at[0, par], partner
        )
        to_partner.start()

        sums = density_of(now)
        for j in range(TILES):
            core_send[par, j : j + 1] = jnp.sum(sums[j], axis=0, keepdims=True)
        core_copy = remote(
            core_send.at[par], core_recv.at[par], send_sem.at[1, par], recv_sem.at[1, par], partner
        )
        core_copy.start()
        core_copy.wait_recv()
        plane_send[par] = core_send[par] + core_recv[par]
        for n, device in enumerate(plane_ids):
            remote(
                plane_send.at[par], plane_recv.at[par, n], send_sem.at[2, par], recv_sem.at[2, par], device
            ).start()

        to_partner.wait_recv()
        rows = []
        for v in range(4):
            own = now[v]
            other = rho_recv[par, v]
            first = jnp.where(core == 0, own, other)
            second = jnp.where(core == 0, other, own)
            rows += [jnp.where(left, first, swap(second)), jnp.where(left, swap(first), second)]
        comps = jnp.concatenate(rows, axis=0)
        blank = jnp.zeros((64, 128), f32)
        messages = dot(couple[0], jnp.concatenate([comps, blank], axis=0), 1, 1)
        messages += dot(couple[1], jnp.concatenate([blank, comps], axis=0), 1, 1)
        for c in range(CHIPS):
            sig_send[par, c] = messages[c * 8 : (c + 1) * 8]
        for n, device in enumerate(plane_ids):
            remote(
                sig_send.at[par, plane_chips[n]],
                sig_recv.at[par, n],
                send_sem.at[3, par],
                recv_sem.at[3, par],
                device,
            ).start()

        wait_bytes(plane_recv.at[par], recv_sem.at[2, par])
        density = plane_send[par]
        for n in range(len(PLANE)):
            density = density + plane_recv[par, n]
        packed = gram_of(coulomb_rows[0:TILES] * density)

        wait_bytes(sig_recv.at[par], recv_sem.at[3, par])
        arrived = sig_send[par, chip]
        for n in range(len(PLANE)):
            arrived = arrived + sig_recv[par, n]
        place_row = iota((8, 128), 0)
        place_lane = lax.rem(iota((8, 128), 1), 64)
        for part in range(2):
            place = (place_lane == place_row * 8 + 2 * ga + part).astype(f32)
            sigma = dot(arrived, place, 0, 0)[part * 64 : part * 64 + 64]
            for v in range(4):
                packed[v] = packed[v] + jnp.where(
                    left, sigma[16 * v : 16 * v + 8], sigma[16 * v + 8 : 16 * v + 16]
                )
        for v in range(4):
            own_terms[par, v] = packed[v]
        for n, device in enumerate(line_ids):
            remote(
                own_terms.at[par], ham_recv.at[par, ga], send_sem.at[4, par], recv_sem.at[4 + n, par], device
            ).start()
        for v in range(4):
            ham_recv[par, ga, v] = packed[v]
        for n in range(3):
            source = lax.rem(ga + SIDE - (n + 1), SIDE)
            wait_bytes(ham_recv.at[par, source], recv_sem.at[4 + n, par])
        field = jnp.float32(0.0)
        for s in range(2 * STEPS):
            field = jnp.where(e == s, jnp.float32(pulse_field(0.5 * time_step * s)), field)
        ham = []
        for v in range(4):
            total = (ham_recv[par, 0, v] + ham_recv[par, 1, v]) + (ham_recv[par, 2, v] + ham_recv[par, 3, v])
            total = total + field * dipole_h[v]
            ham.append(total + band_diag if v == 0 else total)
        change = change_of(ham, [now[0] + ground] + now[1:])
        length = jnp.where(par == 0, jnp.float32(0.5 * time_step), jnp.float32(time_step))
        new = [b + length * c for b, c in zip(base, change)]
        base = [jnp.where(par == 0, b, n) for b, n in zip(base, new)]

        to_partner.wait_send()
        core_copy.wait_send()
        wait_bytes(plane_recv.at[par], send_sem.at[2, par])
        wait_bytes(sig_recv.at[par], send_sem.at[3, par])
        wait_bytes(ham_recv.at[par, pl.ds(0, 3)], send_sem.at[4, par])
        return tuple(base) + tuple(new)

    final = lax.fori_loop(0, 2 * STEPS, evaluate, tuple(start) + tuple(start))[:4]
    rows = []
    for v in range(4):
        rows += [final[v], swap(final[v])]
    out_ref[...] = dot(jnp.concatenate(rows, axis=0), back_buf[...], 0, 0)[:NK]


def local(delta_rho, bloch_blocks, coulomb, energies, dipole, pair_count, pair_target, kernel_list):
    into, back = component_tables()
    hbm = pl.BlockSpec(memory_space=pl.ANY)
    return pl.pallas_call(
        kernel,
        out_shape=jax.ShapeDtypeStruct((NK, 128), f32),
        in_specs=[hbm] * 5 + [pl.BlockSpec(memory_space=pltpu.SMEM)] + [hbm] * 4,
        out_specs=pl.BlockSpec(memory_space=pltpu.VMEM),
        scratch_shapes=[
            pltpu.VMEM((NK, 128), f32),
            pltpu.VMEM((NK, 2, NB, NG), f32),
            pltpu.VMEM((1, NG), f32),
            pltpu.VMEM((NK, NB), f32),
            pltpu.VMEM((NK, 128), f32),
            pltpu.VMEM((16, MAXP), jnp.int32),
            pltpu.VMEM((16, MAXP * KB * KB), f32),
            pltpu.VMEM((64, 128), f32),
            pltpu.VMEM((64, 128), f32),
            pltpu.VMEM((NK * 8, 8, WIDE), f32),
            pltpu.VMEM((NK, 2, 8, 128), f32),
            pltpu.VMEM((64, 8, 128), f32),
            pltpu.VMEM((2, 4, 8, 128), f32),
            pltpu.VMEM((2, 128, 128), f32),
            pltpu.VMEM((16, 128), f32),
            pltpu.VMEM((2, 4, 8, 128), f32),
            pltpu.VMEM((2, 4, 8, 128), f32),
            pltpu.VMEM((2, TILES, 128), f32),
            pltpu.VMEM((2, TILES, 128), f32),
            pltpu.VMEM((2, TILES, 128), f32),
            pltpu.VMEM((2, CHIPS - 1, TILES, 128), f32),
            pltpu.VMEM((2, CHIPS, 8, 128), f32),
            pltpu.VMEM((2, CHIPS - 1, 8, 128), f32),
            pltpu.VMEM((2, SIDE, 4, 8, 128), f32),
            pltpu.SemaphoreType.DMA((8,)),
            pltpu.SemaphoreType.DMA((CHUNKS,)),
            pltpu.SemaphoreType.DMA((5, 2)),
            pltpu.SemaphoreType.DMA((7, 2)),
        ],
        compiler_params=pltpu.CompilerParams(
            collective_id=0, has_side_effects=True, vmem_limit_bytes=52 * 1024 * 1024
        ),
        name="propagate",
    )(
        delta_rho,
        bloch_blocks,
        coulomb.reshape(1, NG),
        energies,
        dipole,
        pair_count,
        pair_target,
        kernel_list,
        jnp.asarray(into),
        jnp.asarray(back),
    )


def solution(mesh):
    in_specs = (
        P("ka", None),
        P("ka", None, None, "ga"),
        P("ga"),
        P("ka", None),
        P("ka", None),
        P(),
        P(),
        P(),
    )
    return jax.shard_map(local, mesh=mesh, in_specs=in_specs, out_specs=P("ka", None), check_vma=False)
```

time: 777 us -> 128 us (0.16)
  blocking collectives: 483 us -> 0 us
  matrix products: 205 us -> 0 us
  Pallas kernels: 0 us -> 119 us
  local copies, waits for them, and re-layouts: 49 us -> 7.65 us
  other arithmetic: 16.6 us -> 0 us
  between operations: 15 us -> 0.03 us
    psum x12 -> x0, blocking collectives: 483 us -> none  [the longest x6 409 us: hartree_local(): density = lax.psum(own_density, 'ka')]
    dot_general x73 -> x0, matrix products: 205 us -> none  [the longest x6 81 us: hartree_local(): jnp.einsum('kag,kbg->kab', orbitals * potential, orbitals, precision=high...]
    pallas_call x0 -> x1, Pallas kernels: none -> 119 us  [local(): pl.pallas_call(kernel, out_shape=jax.ShapeDtypeStruct((NK, 128), f32), in...]
    mul x17 -> x0, local copies, waits for them, and re-layouts: 10.9 us -> none  [the longest x5 4.6 us: local(): time_step * change_of(hamiltonian(half_step, moment + 0.5 * time_step), h...]
    squeeze x15 -> x0, local copies, waits for them, and re-layouts: 9.43 us -> none  [split_parts(): return (pieces[:, 0], pieces[:, 1])]
    add x24 -> x0, other arithmetic: 8.39 us -> none  [the longest x3 2.77 us: local(): half_step + ground]
  transfers between devices with their start and end apart: 6 -> 0, of which waited for: 0 -> 0; matrix products, arithmetic and copies ran while one was open for 22% -> 0% of each run, Pallas kernels for 0% -> 0%
where the time goes in v1:
time: 128 us; the launch traced here: 127 us
  Pallas kernels  119 us (93%)
  local copies, waits for them, and re-layouts  7.65 us (6%)
    pallas_call x1, Pallas kernels, local(): pl.pallas_call(kernel, out_shape=jax.ShapeDtypeStruct((NK, 128), f32), in...  119 us
    unnamed x15, local copies, waits for them, and re-layouts  6.95 us

profile of v1, /device:TPU:1, one launch (start us, length us, event | category | flops | bytes accessed | tf_op | source)
XLA Modules:
  0.0 127.1 jit_solution(5121273805350720374)
XLA Ops:
  0.0 0.7 reshape.3.coulomb_hbm
  0.7 0.8 copy.11.energies_hbm
  1.5 0.8 copy.12.target_hbm
  2.3 0.0 copy-start
  2.3 1.0 copy-done
  3.3 0.0 copy-start.1
  3.3 0.8 copy-done.1
  4.1 0.0 copy-start.2
  4.1 0.8 copy-done.2
  4.9 0.0 copy-start.3
  4.9 0.8 copy-done.3
  5.6 0.0 copy-start.4
  5.6 0.8 copy-done.4
  6.4 0.0 copy-start.5
  6.4 0.7 copy-done.5
  7.1 119.4 %propagate.1 = f32[64,128]{1,0:T(8,128)S(1)} custom-call(f32[64,128]{1,0:T(8,128)S(1)} %copy-done.1, f32[64,2,8,1500]{3,2,1,0:T(8,128)} %bloch_hbm.1, f32[1,1500]{1,0:T(1,128)S(1)} %reshape.3.coulomb_hbm, f32[64,8]{1,0:T(8,128)S(1)} %copy.11.energies_hbm, f32[64,128]{1,0:T(8,128)S(1)} %copy-done.2, s32[256]{0:T(256)S(1)} %copy-done.5, ...), custom_call_target="tpu_custom_call" | custom-call | tf_op jit(solution)/shard_map/propagate/pallas_call | solution.py:454
  126.5 0.6 copy.14
Async XLA Ops:
  2.3 1.0 copy-start
  3.3 0.8 copy-start.1
  4.1 0.8 copy-start.2
  4.9 0.8 copy-start.3
  5.6 0.8 copy-start.4
  6.4 0.7 copy-start.5

commit v2 on v1

v2 whole, which is shorter than its diff:
```python
import functools
import math

import jax
import jax.numpy as jnp
import numpy as np
from jax import lax
from jax.experimental import pallas as pl
from jax.experimental.pallas import tpu as pltpu
from jax.sharding import PartitionSpec as P

NB = 8
KB = 8
MAXP = 8
STEPS = 3
NBLK = 8
NK = 64
NG = 1500
TILES = 12
WIDE = TILES * 128
CHIPS = 16
SIDE = 4
CHUNKS = 8
HALF = TILES // 2
UNROLL = 16

time_step = 0.1
pulse_amp = 3.0
pulse_center = 0.15
pulse_width = 0.2
pulse_freq = 2.0
highest = lax.Precision.HIGHEST
MESH = pl.DeviceIdType.MESH
f32 = jnp.float32


def hops(step):
    return min(step, SIDE - step)


PLANE = sorted(
    [(a, b) for a in range(SIDE) for b in range(SIDE) if (a, b) != (0, 0)],
    key=lambda at: -(hops(at[0]) + hops(at[1])),
)
LINE = (2, 1, 3)


def pulse_field(moment):
    return (
        pulse_amp
        * math.exp(-(((moment - pulse_center) / pulse_width) ** 2))
        * math.cos(pulse_freq * moment)
    )


def component_tables():
    into = np.zeros((64, 128), np.float32)
    back = np.zeros((64, 128), np.float32)

    def real_entry(row, i, j):
        into[row, i * 8 + j] += 0.5
        into[row, j * 8 + i] += 0.5
        back[row, i * 8 + j] = 1.0
        back[row, j * 8 + i] = 1.0

    def imag_entry(row, i, j):
        into[row, 64 + i * 8 + j] += 0.5
        into[row, 64 + j * 8 + i] -= 0.5
        back[row, 64 + i * 8 + j] = 1.0
        back[row, 64 + j * 8 + i] = -1.0

    for i in range(8):
        real_entry(i, i, i)
        if i < 4:
            real_entry(8 + i, i, i + 4)
        else:
            imag_entry(8 + i, i, i - 4)
        for v in (1, 2, 3):
            real_entry(16 * v + i, i, (i + v) % 8)
            imag_entry(16 * v + 8 + i, i, (i + v) % 8)
    return into, back


def dot(a, b, lhs_dim, rhs_dim, precision=highest):
    return lax.dot_general(
        a, b, (((lhs_dim,), (rhs_dim,)), ((), ())), precision=precision, preferred_element_type=f32
    )


def iota(shape, axis):
    return lax.broadcasted_iota(jnp.int32, shape, axis)


def rolled(value, up):
    up = up % 8
    return value if up == 0 else pltpu.roll(value, 8 - up, 0)


def swap(value):
    return pltpu.roll(value, 64, 1)


def unpacked(packed):
    left = iota((8, 128), 1) < 64
    comps = []
    for value in packed:
        other = swap(value)
        comps += [jnp.where(left, value, other), jnp.where(left, other, value)]
    return comps


def offsets_of(comps):
    top = iota((8, 128), 0) < 4
    mixed = comps[1]
    turned = rolled(mixed, 4)
    real = [comps[0], comps[2], comps[4], comps[6], jnp.where(top, mixed, turned)]
    imag = [None, comps[3], comps[5], comps[7], jnp.where(top, -turned, mixed)]
    for offset in (5, 6, 7):
        real.append(rolled(real[8 - offset], offset))
        imag.append(-rolled(imag[8 - offset], offset))
    return real, imag


def change_of(hamilton, state):
    top = iota((8, 128), 0) < 4
    ham_re, ham_im = offsets_of(hamilton)
    rho_re, rho_im = offsets_of(state)

    def add(total, term):
        return term if total is None else total + term

    prod_re, prod_im = [], []
    for d in range(8):
        plus, minus, cross = None, None, None
        for e in range(8):
            f = (d - e) % 8
            re = rolled(rho_re[f], e)
            plus = add(plus, ham_re[e] * re)
            if e > 0:
                cross = add(cross, ham_im[e] * re)
            if f > 0:
                im = rolled(rho_im[f], e)
                cross = add(cross, ham_re[e] * im)
                if e > 0:
                    minus = add(minus, ham_im[e] * im)
        prod_re.append(plus - minus)
        prod_im.append(cross)
    change_re, change_im = [], []
    for d in range(5):
        other = (8 - d) % 8
        change_re.append(prod_im[d] + rolled(prod_im[other], d))
        change_im.append(rolled(prod_re[other], d) - prod_re[d])
    return [
        change_re[0],
        jnp.where(top, change_re[4], change_im[4]),
        change_re[1],
        change_im[1],
        change_re[2],
        change_im[2],
        change_re[3],
        change_im[3],
    ]


def build_pairs(bands, tail, pairs, first, last):
    top = iota((8, 128), 0) < 4

    def build(k, _):
        edge = (TILES - 1) * 128
        for part in range(2):
            tail[k, part, :, : NG - edge] = bands[k, part, :, edge:]
        for j in range(TILES):
            lanes = slice(j * 128, (j + 1) * 128)
            if j < TILES - 1:
                u, v = bands[k, 0, :, lanes], bands[k, 1, :, lanes]
            else:
                u, v = tail[k, 0], tail[k, 1]
            us = [u] + [rolled(u, d) for d in (1, 2, 3, 4)]
            vs = [v] + [rolled(v, d) for d in (1, 2, 3, 4)]
            values = [
                u * u + v * v,
                u * jnp.where(top, us[4], vs[4]) + v * jnp.where(top, vs[4], -us[4]),
            ]
            for d in (1, 2, 3):
                values += [u * us[d] + v * vs[d], u * vs[d] - v * us[d]]
            for t, value in enumerate(values):
                pairs[k * 8 + t, :, lanes] = value
        return 0

    lax.fori_loop(first, last, build, 0)


def density_of(pairs, state, first):
    top = iota((8, 128), 0) < 4
    weights = [state[0], jnp.where(top, 2.0, -2.0) * state[1]]
    for v in (1, 2, 3):
        weights += [2.0 * state[2 * v], -2.0 * state[2 * v + 1]]

    def add(step, sums):
        sums = list(sums)
        for r in range(UNROLL):
            k = step * UNROLL + r
            at = jnp.full((8, 128), k, jnp.int32)
            for t in range(8):
                weight = jnp.take_along_axis(weights[t], at, axis=1, mode="promise_in_bounds")
                for j in range(HALF):
                    lanes = slice((first + j) * 128, (first + j + 1) * 128)
                    sums[j] = sums[j] + weight * pairs[k * 8 + t, :, lanes]
        return tuple(sums)

    return lax.fori_loop(0, NK // UNROLL, add, (jnp.zeros((8, 128), f32),) * HALF)


def gram_of(pairs, rows, first):
    lane = iota((8, 128), 1)
    spread = [jnp.broadcast_to(rows[j : j + 1], (8, 128)) for j in range(HALF)]

    def group(step, packed):
        packed = list(packed)
        for r in range(UNROLL):
            k = step * UNROLL + r
            for t in range(8):
                total = None
                for j in range(HALF):
                    lanes = slice((first + j) * 128, (first + j + 1) * 128)
                    term = spread[j] * pairs[k * 8 + t, :, lanes]
                    total = term if total is None else total + term
                summed = jnp.broadcast_to(jnp.sum(total, axis=1, keepdims=True), (8, 128))
                packed[t // 2] = jnp.where(lane == (t % 2) * 64 + k, summed, packed[t // 2])
        return tuple(packed)

    return lax.fori_loop(0, NK // UNROLL, group, (jnp.zeros((8, 128), f32),) * 4)


def kernel(
    rho_hbm, bloch_hbm, coulomb_hbm, energies_hbm, dipole_hbm, count_hbm, target_hbm, kernel_hbm, into_hbm, back_hbm,
    out_ref,
    rho_buf, bands, coulomb_buf, energies_buf, dipole_buf, count_buf, target_buf, kernel_buf, into_buf, back_buf,
    pairs, tail, couple, coulomb_rows,
    rho_send, rho_recv, core_send, core_recv, plane_send, plane_recv, sig_send, sig_recv, rows_send, rows_recv,
    ham_send, ham_recv,
    load_sem, band_sem, send_sem, recv_sem,
):
    ka = lax.axis_index("ka")
    ga = lax.axis_index("ga")
    core = lax.rem(ka, 2)
    chip = ka // 2
    chip_x = chip // SIDE
    chip_z = lax.rem(chip, SIDE)

    partner = (chip * 2 + (1 - core), ga)
    plane_chips = [
        lax.rem(chip_x + a, SIDE) * SIDE + lax.rem(chip_z + b, SIDE) for a, b in PLANE
    ]
    plane_ids = [(c * 2 + core, ga) for c in plane_chips]
    line_ids = [(ka, lax.rem(ga + d, SIDE)) for d in LINE]
    line_sources = [lax.rem(ga + SIDE - d, SIDE) for d in LINE]

    barrier = pltpu.get_barrier_semaphore()
    everyone = [partner] + plane_ids + line_ids
    for device in everyone:
        pl.semaphore_signal(barrier, inc=1, device_id=device, device_id_type=MESH)

    step_k = NK // CHUNKS
    band_loads = [
        pltpu.make_async_copy(
            bloch_hbm.at[pl.ds(n * step_k, step_k)],
            bands.at[pl.ds(n * step_k, step_k)],
            band_sem.at[n],
        )
        for n in range(CHUNKS)
    ]
    first_block = pl.multiple_of(chip * 16, 16)
    loads = [
        pltpu.make_async_copy(src, dst, load_sem.at[n])
        for n, (src, dst) in enumerate(
            [
                (rho_hbm, rho_buf),
                (into_hbm, into_buf),
                (dipole_hbm, dipole_buf),
                (energies_hbm, energies_buf),
                (coulomb_hbm, coulomb_buf),
                (count_hbm, count_buf),
                (target_hbm, target_buf),
                (kernel_hbm.at[pl.ds(first_block, 16)], kernel_buf),
                (back_hbm, back_buf),
            ]
        )
    ]
    for copy in loads:
        copy.start()
    for copy in band_loads:
        copy.start()

    lane = iota((8, 128), 1)
    row = iota((8, 128), 0)
    left = lane < 64
    top = row < 4

    tail[...] = jnp.zeros((NK, 2, 8, 128), f32)
    coulomb_rows[...] = jnp.zeros((2, 8, 128), f32)
    core_send[...] = jnp.zeros((2, 2, 8, 128), f32)

    for copy in loads:
        copy.wait()

    def components(rows):
        comps = dot(into_buf[...], jnp.concatenate([rows, rows], axis=0), 1, 1)
        return [comps[8 * t : 8 * t + 8] for t in range(8)]

    start = components(rho_buf[...])
    dipole_h = components(dipole_buf[...])
    band_diag = jnp.concatenate([energies_buf[...]] * 2, axis=1)
    ground = jnp.where(top, 1.0, 0.0)

    for j in range(TILES):
        width = min(128, NG - j * 128)
        coulomb_rows[j // HALF, j % HALF : j % HALF + 1, 0:width] = (
            coulomb_buf[j * 128 : j * 128 + width].reshape(1, width) * (1.0 / 2048.0)
        )

    chosen = (iota((256, 128), 0) == chip * 16 + lax.rem(iota((256, 128), 1), 16)).astype(f32)
    wide_target = dot(target_buf[...].astype(f32), chosen, 1, 0)
    target_line = jnp.sum(jnp.where(lane // 16 == row, wide_target, 0.0), axis=0, keepdims=True)
    counts = jnp.broadcast_to(count_buf[...].astype(f32).reshape(1, 256), (8, 256))
    live = (iota((1, 128), 1) // 16).astype(f32) < dot(counts, chosen, 1, 0)[0:1]
    wide_row = iota((128, 128), 0)
    wide_lane = iota((128, 128), 1)
    block_of_row = ((wide_row // 8) * 2 + core) * 8 + lax.rem(wide_row, 8)
    line = jnp.where(live, target_line, -1.0)
    hot = (line == block_of_row.astype(f32)).astype(f32)
    entry_rows = jnp.concatenate(
        [kernel_buf[:, p * 64 : (p + 1) * 64] for p in range(MAXP)], axis=0
    )
    for part in range(2):
        pick_row = iota((64, 128), 0)
        pick = (pick_row // 8 == 2 * ga + part) & (
            lax.rem(pick_row, 8) == lax.rem(iota((64, 128), 1), 8)
        )
        spread_rows = dot(entry_rows, pick.astype(f32), 1, 0)
        spread_rows = jnp.where(lax.rem(wide_row, 16) == wide_lane // 8, spread_rows, 0.0)
        couple[part] = -dot(hot, spread_rows, 1, 0)

    for n, copy in enumerate(band_loads):
        copy.wait()
        build_pairs(bands, tail, pairs, n * step_k, (n + 1) * step_k)

    def remote(src, dst, send, recv, device):
        return pltpu.make_async_remote_copy(
            src_ref=src, dst_ref=dst, send_sem=send, recv_sem=recv, device_id=device, device_id_type=MESH
        )

    def wait_bytes(ref, sem):
        pltpu.make_async_copy(ref, ref, sem).wait()

    pl.semaphore_wait(barrier, len(everyone))

    def evaluate(e, carry):
        base, now = list(carry[:8]), list(carry[8:])
        par = lax.rem(e, 2)
        for v in range(4):
            rho_send[par, v] = jnp.where(left, now[2 * v], now[2 * v + 1])
        to_partner = remote(
            rho_send.at[par], rho_recv.at[par], send_sem.at[0, par], recv_sem.at[0, par], partner
        )
        to_partner.start()

        core_copies = []
        for half in range(2):
            sums = density_of(pairs, now, half * HALF)
            for j in range(HALF):
                core_send[par, half, j : j + 1] = jnp.sum(sums[j], axis=0, keepdims=True)
            core_copies.append(
                remote(
                    core_send.at[par, half],
                    core_recv.at[par, half],
                    send_sem.at[1 + half, par],
                    recv_sem.at[1 + half, par],
                    partner,
                )
            )
            core_copies[half].start()

        def to_plane(half):
            core_copies[half].wait_recv()
            plane_send[par, half] = core_send[par, half] + core_recv[par, half]
            for n, device in enumerate(plane_ids):
                remote(
                    plane_send.at[par, half],
                    plane_recv.at[par, half, n],
                    send_sem.at[3 + half, par],
                    recv_sem.at[3 + half, par],
                    device,
                ).start()

        to_plane(0)

        to_partner.wait_recv()
        others = unpacked([rho_recv[par, v] for v in range(4)])
        first_core = core == 0
        rows = []
        for t in range(8):
            first = jnp.where(first_core, now[t], others[t])
            second = jnp.where(first_core, others[t], now[t])
            rows.append(jnp.where(left, first, second))
        comps = jnp.concatenate(rows, axis=0)
        blank = jnp.zeros((64, 128), f32)
        messages = dot(couple[0], jnp.concatenate([comps, blank], axis=0), 1, 1)
        messages += dot(couple[1], jnp.concatenate([blank, comps], axis=0), 1, 1)
        for c in range(CHIPS):
            sig_send[par, c] = messages[c * 8 : (c + 1) * 8]
        for n, device in enumerate(plane_ids):
            remote(
                sig_send.at[par, plane_chips[n]],
                sig_recv.at[par, n],
                send_sem.at[5, par],
                recv_sem.at[5, par],
                device,
            ).start()

        to_plane(1)

        def potential_of(half):
            wait_bytes(plane_recv.at[par, half], recv_sem.at[3 + half, par])
            density = plane_send[par, half]
            for n in range(len(PLANE)):
                density = density + plane_recv[par, half, n]
            return coulomb_rows[half] * density

        packed = gram_of(pairs, potential_of(0), 0)

        wait_bytes(sig_recv.at[par], recv_sem.at[5, par])
        arrived = sig_send[par, chip]
        for n in range(len(PLANE)):
            arrived = arrived + sig_recv[par, n]
        rows_send[par] = arrived
        for n, device in enumerate(line_ids):
            remote(
                rows_send.at[par], rows_recv.at[par, ga], send_sem.at[6, par], recv_sem.at[6 + n, par], device
            ).start()
        rows_recv[par, ga] = arrived

        second = gram_of(pairs, potential_of(1), HALF)
        packed = [a + b for a, b in zip(packed, second)]
        for v in range(4):
            ham_send[par, v] = packed[v]
        for n, device in enumerate(line_ids):
            remote(
                ham_send.at[par], ham_recv.at[par, ga], send_sem.at[7, par], recv_sem.at[9 + n, par], device
            ).start()
        for v in range(4):
            ham_recv[par, ga, v] = packed[v]

        for n, source in enumerate(line_sources):
            wait_bytes(rows_recv.at[par, source], recv_sem.at[6 + n, par])
        all_rows = jnp.concatenate([rows_recv[par, g] for g in range(SIDE)], axis=0)
        place_row = iota((32, 128), 0)
        place_lane = lax.rem(iota((32, 128), 1), 64)
        sigma = None
        for part in range(2):
            at = lax.rem(place_row, 8) * 8 + 2 * (place_row // 8) + part
            placed = dot(all_rows, (place_lane == at).astype(f32), 0, 0)[part * 64 : part * 64 + 64]
            sigma = placed if sigma is None else sigma + placed
        field = jnp.float32(0.0)
        for s in range(2 * STEPS):
            field = jnp.where(e == s, jnp.float32(pulse_field(0.5 * time_step * s)), field)
        known = [sigma[8 * t : 8 * t + 8] + field * dipole_h[t] for t in range(8)]
        known[0] = known[0] + band_diag

        for n, source in enumerate(line_sources):
            wait_bytes(ham_recv.at[par, source], recv_sem.at[9 + n, par])
        hartree = unpacked(
            [
                (ham_recv[par, 0, v] + ham_recv[par, 1, v]) + (ham_recv[par, 2, v] + ham_recv[par, 3, v])
                for v in range(4)
            ]
        )
        ham = [h + other for h, other in zip(hartree, known)]
        change = change_of(ham, [now[0] + ground] + now[1:])
        length = jnp.where(par == 0, jnp.float32(0.5 * time_step), jnp.float32(time_step))
        new = [b + length * c for b, c in zip(base, change)]
        base = [jnp.where(par == 0, b, n) for b, n in zip(base, new)]

        to_partner.wait_send()
        for half in range(2):
            core_copies[half].wait_send()
            wait_bytes(plane_recv.at[par, half], send_sem.at[3 + half, par])
        wait_bytes(sig_recv.at[par], send_sem.at[5, par])
        wait_bytes(rows_recv.at[par, pl.ds(0, 3)], send_sem.at[6, par])
        wait_bytes(ham_recv.at[par, pl.ds(0, 3)], send_sem.at[7, par])
        return tuple(base) + tuple(new)

    final = lax.fori_loop(0, 2 * STEPS, evaluate, tuple(start) + tuple(start))[:8]
    out_ref[...] = dot(jnp.concatenate(final, axis=0), back_buf[...], 0, 0)[:NK]


def local(delta_rho, bloch_blocks, coulomb, energies, dipole, pair_count, pair_target, kernel_list):
    into, back = component_tables()
    hbm = pl.BlockSpec(memory_space=pltpu.HBM)
    return pl.pallas_call(
        kernel,
        out_shape=jax.ShapeDtypeStruct((NK, 128), f32),
        in_specs=[hbm] * 10,
        out_specs=pl.BlockSpec(memory_space=pltpu.VMEM),
        scratch_shapes=[
            pltpu.VMEM((NK, 128), f32),
            pltpu.VMEM((NK, 2, NB, NG), f32),
            pltpu.VMEM((NG,), f32),
            pltpu.VMEM((NB, NK), f32),
            pltpu.VMEM((NK, 128), f32),
            pltpu.VMEM((256,), jnp.int32),
            pltpu.VMEM((MAXP, 256), jnp.int32),
            pltpu.VMEM((16, MAXP * KB * KB), f32),
            pltpu.VMEM((64, 128), f32),
            pltpu.VMEM((64, 128), f32),
            pltpu.VMEM((NK * 8, 8, WIDE), f32),
            pltpu.VMEM((NK, 2, 8, 128), f32),
            pltpu.VMEM((2, 128, 128), f32),
            pltpu.VMEM((2, 8, 128), f32),
            pltpu.VMEM((2, 4, 8, 128), f32),
            pltpu.VMEM((2, 4, 8, 128), f32),
            pltpu.VMEM((2, 2, 8, 128), f32),
            pltpu.VMEM((2, 2, 8, 128), f32),
            pltpu.VMEM((2, 2, 8, 128), f32),
            pltpu.VMEM((2, 2, CHIPS - 1, 8, 128), f32),
            pltpu.VMEM((2, CHIPS, 8, 128), f32),
            pltpu.VMEM((2, CHIPS - 1, 8, 128), f32),
            pltpu.VMEM((2, 8, 128), f32),
            pltpu.VMEM((2, SIDE, 8, 128), f32),
            pltpu.VMEM((2, 4, 8, 128), f32),
            pltpu.VMEM((2, SIDE, 4, 8, 128), f32),
            pltpu.SemaphoreType.DMA((9,)),
            pltpu.SemaphoreType.DMA((CHUNKS,)),
            pltpu.SemaphoreType.DMA((8, 2)),
            pltpu.SemaphoreType.DMA((12, 2)),
        ],
        compiler_params=pltpu.CompilerParams(
            collective_id=0, has_side_effects=True, vmem_limit_bytes=58 * 1024 * 1024
        ),
        name="propagate",
    )(
        delta_rho,
        bloch_blocks,
        coulomb,
        energies.T,
        dipole,
        pair_count,
        pair_target.T,
        kernel_list,
        jnp.asarray(into),
        jnp.asarray(back),
    )


def solution(mesh):
    in_specs = (
        P("ka", None),
        P("ka", None, None, "ga"),
        P("ga"),
        P("ka", None),
        P("ka", None),
        P(),
        P(),
        P(),
    )
    return jax.shard_map(local, mesh=mesh, in_specs=in_specs, out_specs=P("ka", None), check_vma=False)
```

time: 128 us -> 92.4 us (0.72)
  Pallas kernels: 119 us -> 90.3 us
  local copies, waits for them, and re-layouts: 7.65 us -> 1.38 us
    pallas_call x1, Pallas kernels: 119 us -> 90.3 us  [local(): pl.pallas_call(kernel, out_shape=jax.ShapeDtypeStruct((NK, 128), f32), in...]
    unnamed x15 -> x1, local copies, waits for them, and re-layouts: 6.95 us -> 1.38 us
where the time goes in v2:
time: 92.4 us; the launch traced here: 91.7 us
  Pallas kernels  90.3 us (98%)
  local copies, waits for them, and re-layouts  1.38 us (1%)
    pallas_call x1, Pallas kernels, local(): pl.pallas_call(kernel, out_shape=jax.ShapeDtypeStruct((NK, 128), f32), in...  90.3 us

profile of v2, /device:TPU:1, one launch (start us, length us, event | category | flops | bytes accessed | tf_op | source)
XLA Modules:
  0.0 91.7 jit_solution(12307904759372679325)
XLA Ops:
  0.0 90.3 %propagate.1 = f32[64,128]{1,0:T(8,128)} custom-call(f32[64,128]{1,0:T(8,128)} %rho_hbm.1, f32[64,2,8,1500]{3,2,1,0:T(8,128)} %bloch_hbm.1, f32[1500]{0:T(1024)} %coulomb_hbm.1, f32[8,64]{1,0:T(8,128)} %bitcast.3, f32[64,128]{1,0:T(8,128)} %dipole_hbm.1, s32[256]{0:T(256)} %count_hbm.1, s32[8,256]{1,0:T(8,128)} %bitcast.2, f32[256,512]{1,0:T(8,128)} %kernel_hbm.1, ...), custom_call_target="tpu_custom_call" | custom-call | tf_op jit(solution)/shard_map/propagate/pallas_call | solution.py:500
  90.3 1.4 %copy.12 = f32[64,128]{1,0:T(8,128)} copy(f32[64,128]{1,0:T(8,128)} %propagate.1) | data formatting | bytes 65536

commit v3 on v2

--- a/solution.py
+++ b/solution.py
@@ -17,12 +17,10 @@
 NK = 64
 NG = 1500
 TILES = 12
-WIDE = TILES * 128
-CHIPS = 16
 SIDE = 4
 CHUNKS = 8
 HALF = TILES // 2
-UNROLL = 16
+UNROLL = 64
 
 time_step = 0.1
 pulse_amp = 3.0
@@ -38,10 +36,9 @@
     return min(step, SIDE - step)
 
 
-PLANE = sorted(
-    [(a, b) for a in range(SIDE) for b in range(SIDE) if (a, b) != (0, 0)],
-    key=lambda at: -(hops(at[0]) + hops(at[1])),
-)
+LAYER = [(a, b, c) for a in range(SIDE) for b in range(SIDE) for c in range(2)]
+DEVICES = len(LAYER)
+ORDER = sorted(range(1, DEVICES), key=lambda n: -(hops(LAYER[n][0]) + hops(LAYER[n][1])))
 LINE = (2, 1, 3)
 
 
@@ -184,13 +181,17 @@
             for d in (1, 2, 3):
                 values += [u * us[d] + v * vs[d], u * vs[d] - v * us[d]]
             for t, value in enumerate(values):
-                pairs[k * 8 + t, :, lanes] = value
+                pairs[j // HALF, k * 8 + t, :, (j % HALF) * 128 : (j % HALF + 1) * 128] = value
         return 0
 
     lax.fori_loop(first, last, build, 0)
 
 
-def density_of(pairs, state, first):
+def loop(body, carry):
+    return body(0, carry) if UNROLL == NK else lax.fori_loop(0, NK // UNROLL, body, carry)
+
+
+def density_of(pairs, state, half):
     top = iota((8, 128), 0) < 4
     weights = [state[0], jnp.where(top, 2.0, -2.0) * state[1]]
     for v in (1, 2, 3):
@@ -204,14 +205,13 @@
             for t in range(8):
                 weight = jnp.take_along_axis(weights[t], at, axis=1, mode="promise_in_bounds")
                 for j in range(HALF):
-                    lanes = slice((first + j) * 128, (first + j + 1) * 128)
-                    sums[j] = sums[j] + weight * pairs[k * 8 + t, :, lanes]
+                    sums[j] = sums[j] + weight * pairs[half, k * 8 + t, :, j * 128 : (j + 1) * 128]
         return tuple(sums)
 
-    return lax.fori_loop(0, NK // UNROLL, add, (jnp.zeros((8, 128), f32),) * HALF)
-
-
-def gram_of(pairs, rows, first):
+    return loop(add, (jnp.zeros((8, 128), f32),) * HALF)
+
+
+def gram_of(pairs, rows, half):
     lane = iota((8, 128), 1)
     spread = [jnp.broadcast_to(rows[j : j + 1], (8, 128)) for j in range(HALF)]
 
@@ -222,14 +222,13 @@
             for t in range(8):
                 total = None
                 for j in range(HALF):
-                    lanes = slice((first + j) * 128, (first + j + 1) * 128)
-                    term = spread[j] * pairs[k * 8 + t, :, lanes]
+                    term = spread[j] * pairs[half, k * 8 + t, :, j * 128 : (j + 1) * 128]
                     total = term if total is None else total + term
                 summed = jnp.broadcast_to(jnp.sum(total, axis=1, keepdims=True), (8, 128))
                 packed[t // 2] = jnp.where(lane == (t % 2) * 64 + k, summed, packed[t // 2])
         return tuple(packed)
 
-    return lax.fori_loop(0, NK // UNROLL, group, (jnp.zeros((8, 128), f32),) * 4)
+    return loop(group, (jnp.zeros((8, 128), f32),) * 4)
 
 
 def kernel(
@@ -237,7 +236,7 @@
     out_ref,
     rho_buf, bands, coulomb_buf, energies_buf, dipole_buf, count_buf, target_buf, kernel_buf, into_buf, back_buf,
     pairs, tail, couple, coulomb_rows,
-    rho_send, rho_recv, core_send, core_recv, plane_send, plane_recv, sig_send, sig_recv, rows_send, rows_recv,
+    place, first_send, first_recv, second_send, second_recv, rows_send, rows_recv,
     ham_send, ham_recv,
     load_sem, band_sem, send_sem, recv_sem,
 ):
@@ -248,16 +247,15 @@
     chip_x = chip // SIDE
     chip_z = lax.rem(chip, SIDE)
 
-    partner = (chip * 2 + (1 - core), ga)
-    plane_chips = [
-        lax.rem(chip_x + a, SIDE) * SIDE + lax.rem(chip_z + b, SIDE) for a, b in PLANE
-    ]
-    plane_ids = [(c * 2 + core, ga) for c in plane_chips]
+    def layer_device(a, b, c):
+        return (lax.rem(chip_x + a, SIDE) * SIDE + lax.rem(chip_z + b, SIDE)) * 2 + lax.rem(core + c, 2)
+
+    layer_ids = [(layer_device(*offset), ga) for offset in LAYER]
     line_ids = [(ka, lax.rem(ga + d, SIDE)) for d in LINE]
     line_sources = [lax.rem(ga + SIDE - d, SIDE) for d in LINE]
 
     barrier = pltpu.get_barrier_semaphore()
-    everyone = [partner] + plane_ids + line_ids
+    everyone = layer_ids[1:] + line_ids
     for device in everyone:
         pl.semaphore_signal(barrier, inc=1, device_id=device, device_id_type=MESH)
 
@@ -270,7 +268,7 @@
         )
         for n in range(CHUNKS)
     ]
-    first_block = pl.multiple_of(chip * 16, 16)
+    first_block = pl.multiple_of(ka * NBLK, NBLK)
     loads = [
         pltpu.make_async_copy(src, dst, load_sem.at[n])
         for n, (src, dst) in enumerate(
@@ -282,7 +280,7 @@
                 (coulomb_hbm, coulomb_buf),
                 (count_hbm, count_buf),
                 (target_hbm, target_buf),
-                (kernel_hbm.at[pl.ds(first_block, 16)], kernel_buf),
+                (kernel_hbm.at[pl.ds(first_block, NBLK)], kernel_buf),
                 (back_hbm, back_buf),
             ]
         )
@@ -299,7 +297,6 @@
 
     tail[...] = jnp.zeros((NK, 2, 8, 128), f32)
     coulomb_rows[...] = jnp.zeros((2, 8, 128), f32)
-    core_send[...] = jnp.zeros((2, 2, 8, 128), f32)
 
     for copy in loads:
         copy.wait()
@@ -319,27 +316,66 @@
             coulomb_buf[j * 128 : j * 128 + width].reshape(1, width) * (1.0 / 2048.0)
         )
 
-    chosen = (iota((256, 128), 0) == chip * 16 + lax.rem(iota((256, 128), 1), 16)).astype(f32)
-    wide_target = dot(target_buf[...].astype(f32), chosen, 1, 0)
-    target_line = jnp.sum(jnp.where(lane // 16 == row, wide_target, 0.0), axis=0, keepdims=True)
-    counts = jnp.broadcast_to(count_buf[...].astype(f32).reshape(1, 256), (8, 256))
-    live = (iota((1, 128), 1) // 16).astype(f32) < dot(counts, chosen, 1, 0)[0:1]
-    wide_row = iota((128, 128), 0)
-    wide_lane = iota((128, 128), 1)
-    block_of_row = ((wide_row // 8) * 2 + core) * 8 + lax.rem(wide_row, 8)
-    line = jnp.where(live, target_line, -1.0)
-    hot = (line == block_of_row.astype(f32)).astype(f32)
+    def exact(a, b, lhs_dim, rhs_dim):
+        return dot(a.astype(f32), b.astype(f32), lhs_dim, rhs_dim)
+
+    target = target_buf[...]
+    blocks = iota((8, 256), 1)
+    counts = jnp.broadcast_to(count_buf[...].reshape(1, 256), (8, 256))
+    live = iota((8, 256), 0) < counts
+    wide_row = iota((256, 256), 0)
+    wide_lane = iota((256, 256), 1)
+    same = wide_row // 8 == wide_lane // 8
+    before = same & (wide_row < wide_lane)
+    lower = iota((8, 8), 1) < iota((8, 8), 0)
+
+    own_block = (iota((256, 128), 0) == ka * 8 + lax.rem(iota((256, 128), 1), 8)) & (iota((256, 128), 1) < 64)
+    on_p = row == lane // 8
+    line = jnp.sum(
+        jnp.where(on_p, exact(jnp.where(live, target // 8, -1), own_block, 1, 0), 0.0), axis=0, keepdims=True
+    )
+    square_row = iota((128, 128), 0)
+    square_lane = iota((128, 128), 1)
+    square = jnp.broadcast_to(line, (128, 128))
+    column = jnp.sum(jnp.where(square_row == square_lane, square, 0.0), axis=1, keepdims=True)
+    rank = jnp.sum(
+        jnp.where((column == square) & (square_row < square_lane), 1.0, 0.0), axis=0, keepdims=True
+    )
+    to = iota((256, 128), 0) // 8
+    to_device = (
+        lax.rem(chip_x + to // 8, SIDE) * SIDE + lax.rem(chip_z + lax.rem(to // 2, SIDE), SIDE)
+    ) * 2 + lax.rem(core + lax.rem(to, 2), 2)
+    slot = (lax.rem(iota((256, 128), 0), 8) - HALF).astype(f32)
+    hot = (line == to_device.astype(f32)) & (rank == slot) & (iota((256, 128), 1) < 64)
     entry_rows = jnp.concatenate(
-        [kernel_buf[:, p * 64 : (p + 1) * 64] for p in range(MAXP)], axis=0
+        [kernel_buf[:, p * 64 : (p + 1) * 64] for p in range(MAXP)] + [jnp.zeros((64, 64), f32)], axis=0
     )
     for part in range(2):
         pick_row = iota((64, 128), 0)
         pick = (pick_row // 8 == 2 * ga + part) & (
             lax.rem(pick_row, 8) == lax.rem(iota((64, 128), 1), 8)
         )
-        spread_rows = dot(entry_rows, pick.astype(f32), 1, 0)
-        spread_rows = jnp.where(lax.rem(wide_row, 16) == wide_lane // 8, spread_rows, 0.0)
-        couple[part] = -dot(hot, spread_rows, 1, 0)
+        spread_rows = exact(entry_rows, pick, 1, 0)
+        keep = (lax.rem(square_row, 8) == square_lane // 8) & (square_lane < 64)
+        couple[part] = -exact(hot, jnp.where(keep, spread_rows, 0.0), 1, 0)
+
+    mine = live & (target // 8 == ka)
+    mine_f = mine.astype(f32)
+    ranks = exact(mine, before, 1, 0) + exact(exact(lower, mine, 1, 0), same, 1, 0)
+    source = wide_lane // 8
+    source_device = (
+        lax.rem(chip_x + SIDE - source // 8, SIDE) * SIDE + lax.rem(chip_z + SIDE - lax.rem(source // 2, SIDE), SIDE)
+    ) * 2 + lax.rem(core + lax.rem(source, 2), 2)
+    placed = jnp.zeros((8, 256), f32)
+    for number in range(2):
+        of_slot = jnp.where(ranks == number, mine_f, 0.0)
+        by_block = jnp.zeros((8, 256), f32)
+        for q in range(8):
+            found = jnp.sum(jnp.where(lax.rem(target, 8) == q, of_slot, 0.0), axis=0, keepdims=True)
+            by_block = jnp.where(iota((8, 256), 0) == q, found, by_block)
+        into_column = (wide_row // 8 == source_device) & (lax.rem(wide_lane, 8) == HALF + number)
+        placed = placed + exact(by_block, into_column, 1, 0)
+    place[...] = placed
 
     for n, copy in enumerate(band_loads):
         copy.wait()
@@ -358,101 +394,64 @@
     def evaluate(e, carry):
         base, now = list(carry[:8]), list(carry[8:])
         par = lax.rem(e, 2)
-        for v in range(4):
-            rho_send[par, v] = jnp.where(left, now[2 * v], now[2 * v + 1])
-        to_partner = remote(
-            rho_send.at[par], rho_recv.at[par], send_sem.at[0, par], recv_sem.at[0, par], partner
-        )
-        to_partner.start()
-
-        core_copies = []
-        for half in range(2):
-            sums = density_of(pairs, now, half * HALF)
-            for j in range(HALF):
-                core_send[par, half, j : j + 1] = jnp.sum(sums[j], axis=0, keepdims=True)
-            core_copies.append(
-                remote(
-                    core_send.at[par, half],
-                    core_recv.at[par, half],
-                    send_sem.at[1 + half, par],
-                    recv_sem.at[1 + half, par],
-                    partner,
-                )
-            )
-            core_copies[half].start()
-
-        def to_plane(half):
-            core_copies[half].wait_recv()
-            plane_send[par, half] = core_send[par, half] + core_recv[par, half]
-            for n, device in enumerate(plane_ids):
-                remote(
-                    plane_send.at[par, half],
-                    plane_recv.at[par, half, n],
-                    send_sem.at[3 + half, par],
-                    recv_sem.at[3 + half, par],
-                    device,
-                ).start()
-
-        to_plane(0)
-
-        to_partner.wait_recv()
-        others = unpacked([rho_recv[par, v] for v in range(4)])
-        first_core = core == 0
-        rows = []
-        for t in range(8):
-            first = jnp.where(first_core, now[t], others[t])
-            second = jnp.where(first_core, others[t], now[t])
-            rows.append(jnp.where(left, first, second))
-        comps = jnp.concatenate(rows, axis=0)
+        comps = jnp.concatenate(now, axis=0)
         blank = jnp.zeros((64, 128), f32)
-        messages = dot(couple[0], jnp.concatenate([comps, blank], axis=0), 1, 1)
-        messages += dot(couple[1], jnp.concatenate([blank, comps], axis=0), 1, 1)
-        for c in range(CHIPS):
-            sig_send[par, c] = messages[c * 8 : (c + 1) * 8]
-        for n, device in enumerate(plane_ids):
+        products = dot(couple[0], jnp.concatenate([comps, blank], axis=0), 1, 1)
+        products += dot(couple[1], jnp.concatenate([blank, comps], axis=0), 1, 1)
+
+        sums = density_of(pairs, now, 0)
+        tile = jnp.zeros((8, 128), f32)
+        for j in range(HALF):
+            tile = jnp.where(row == j, jnp.sum(sums[j], axis=0, keepdims=True), tile)
+        first_recv[par, 0] = tile + products[0:8]
+        for n in ORDER:
+            first_send[par, n] = tile + products[8 * n : 8 * n + 8]
+        for n in ORDER:
             remote(
-                sig_send.at[par, plane_chips[n]],
-                sig_recv.at[par, n],
-                send_sem.at[5, par],
-                recv_sem.at[5, par],
-                device,
+                first_send.at[par, n], first_recv.at[par, n], send_sem.at[0, par], recv_sem.at[0, par], layer_ids[n]
             ).start()
 
-        to_plane(1)
-
-        def potential_of(half):
-            wait_bytes(plane_recv.at[par, half], recv_sem.at[3 + half, par])
-            density = plane_send[par, half]
-            for n in range(len(PLANE)):
-                density = density + plane_recv[par, half, n]
-            return coulomb_rows[half] * density
-
-        packed = gram_of(pairs, potential_of(0), 0)
-
-        wait_bytes(sig_recv.at[par], recv_sem.at[5, par])
-        arrived = sig_send[par, chip]
-        for n in range(len(PLANE)):
-            arrived = arrived + sig_recv[par, n]
+        sums = density_of(pairs, now, 1)
+        for j in range(HALF):
+            second_send[par, j : j + 1] = jnp.sum(sums[j], axis=0, keepdims=True)
+        for n in ORDER:
+            remote(
+                second_send.at[par], second_recv.at[par, n], send_sem.at[1, par], recv_sem.at[1, par], layer_ids[n]
+            ).start()
+        second_recv[par, 0] = second_send[par]
+
+        def total_of(parts):
+            while len(parts) > 1:
+                parts = [a + b for a, b in zip(parts[0::2], parts[1::2])]
+            return parts[0]
+
+        wait_bytes(first_recv.at[par, pl.ds(1, DEVICES - 1)], recv_sem.at[0, par])
+        density = total_of([first_recv[par, n] for n in range(DEVICES)])
+        arrived = dot(place[...], first_recv[par].reshape(DEVICES * 8, 128), 1, 0)
+        packed = gram_of(pairs, coulomb_rows[0] * density, 0)
+
         rows_send[par] = arrived
         for n, device in enumerate(line_ids):
             remote(
-                rows_send.at[par], rows_recv.at[par, ga], send_sem.at[6, par], recv_sem.at[6 + n, par], device
+                rows_send.at[par], rows_recv.at[par, ga], send_sem.at[2, par], recv_sem.at[2 + n, par], device
             ).start()
         rows_recv[par, ga] = arrived
 
-        second = gram_of(pairs, potential_of(1), HALF)
+        wait_bytes(second_recv.at[par, pl.ds(1, DEVICES - 1)], recv_sem.at[1, par])
+        density = total_of([second_recv[par, n] for n in range(DEVICES)])
+        second = gram_of(pairs, coulomb_rows[1, 0:HALF] * density, 1)
         packed = [a + b for a, b in zip(packed, second)]
         for v in range(4):
             ham_send[par, v] = packed[v]
         for n, device in enumerate(line_ids):
             remote(
-                ham_send.at[par], ham_recv.at[par, ga], send_sem.at[7, par], recv_sem.at[9 + n, par], device
+                ham_send.at[par], ham_recv.at[par, ga], send_sem.at[3, par], recv_sem.at[5 + n, par], device
             ).start()
         for v in range(4):
             ham_recv[par, ga, v] = packed[v]
 
         for n, source in enumerate(line_sources):
-            wait_bytes(rows_recv.at[par, source], recv_sem.at[6 + n, par])
+            wait_bytes(rows_recv.at[par, source], recv_sem.at[2 + n, par])
         all_rows = jnp.concatenate([rows_recv[par, g] for g in range(SIDE)], axis=0)
         place_row = iota((32, 128), 0)
         place_lane = lax.rem(iota((32, 128), 1), 64)
@@ -468,7 +467,7 @@
         known[0] = known[0] + band_diag
 
         for n, source in enumerate(line_sources):
-            wait_bytes(ham_recv.at[par, source], recv_sem.at[9 + n, par])
+            wait_bytes(ham_recv.at[par, source], recv_sem.at[5 + n, par])
         hartree = unpacked(
             [
                 (ham_recv[par, 0, v] + ham_recv[par, 1, v]) + (ham_recv[par, 2, v] + ham_recv[par, 3, v])
@@ -481,13 +480,10 @@
         new = [b + length * c for b, c in zip(base, change)]
         base = [jnp.where(par == 0, b, n) for b, n in zip(base, new)]
 
-        to_partner.wait_send()
-        for half in range(2):
-            core_copies[half].wait_send()
-            wait_bytes(plane_recv.at[par, half], send_sem.at[3 + half, par])
-        wait_bytes(sig_recv.at[par], send_sem.at[5, par])
-        wait_bytes(rows_recv.at[par, pl.ds(0, 3)], send_sem.at[6, par])
-        wait_bytes(ham_recv.at[par, pl.ds(0, 3)], send_sem.at[7, par])
+        wait_bytes(first_recv.at[par, pl.ds(1, DEVICES - 1)], send_sem.at[0, par])
+        wait_bytes(second_recv.at[par, pl.ds(1, DEVICES - 1)], send_sem.at[1, par])
+        wait_bytes(rows_recv.at[par, pl.ds(0, 3)], send_sem.at[2, par])
+        wait_bytes(ham_recv.at[par, pl.ds(0, 3)], send_sem.at[3, par])
         return tuple(base) + tuple(new)
 
     final = lax.fori_loop(0, 2 * STEPS, evaluate, tuple(start) + tuple(start))[:8]
@@ -510,29 +506,26 @@
             pltpu.VMEM((NK, 128), f32),
             pltpu.VMEM((256,), jnp.int32),
             pltpu.VMEM((MAXP, 256), jnp.int32),
-            pltpu.VMEM((16, MAXP * KB * KB), f32),
+            pltpu.VMEM((NBLK, MAXP * KB * KB), f32),
             pltpu.VMEM((64, 128), f32),
             pltpu.VMEM((64, 128), f32),
-            pltpu.VMEM((NK * 8, 8, WIDE), f32),
+            pltpu.VMEM((2, NK * 8, 8, HALF * 128), f32),
             pltpu.VMEM((NK, 2, 8, 128), f32),
-            pltpu.VMEM((2, 128, 128), f32),
+            pltpu.VMEM((2, 256, 128), f32),
             pltpu.VMEM((2, 8, 128), f32),
-            pltpu.VMEM((2, 4, 8, 128), f32),
-            pltpu.VMEM((2, 4, 8, 128), f32),
-            pltpu.VMEM((2, 2, 8, 128), f32),
-            pltpu.VMEM((2, 2, 8, 128), f32),
-            pltpu.VMEM((2, 2, 8, 128), f32),
-            pltpu.VMEM((2, 2, CHIPS - 1, 8, 128), f32),
-            pltpu.VMEM((2, CHIPS, 8, 128), f32),
-            pltpu.VMEM((2, CHIPS - 1, 8, 128), f32),
+            pltpu.VMEM((8, DEVICES * 8), f32),
+            pltpu.VMEM((2, DEVICES, 8, 128), f32),
+            pltpu.VMEM((2, DEVICES, 8, 128), f32),
+            pltpu.VMEM((2, HALF, 128), f32),
+            pltpu.VMEM((2, DEVICES, HALF, 128), f32),
             pltpu.VMEM((2, 8, 128), f32),
             pltpu.VMEM((2, SIDE, 8, 128), f32),
             pltpu.VMEM((2, 4, 8, 128), f32),
             pltpu.VMEM((2, SIDE, 4, 8, 128), f32),
             pltpu.SemaphoreType.DMA((9,)),
             pltpu.SemaphoreType.DMA((CHUNKS,)),
+            pltpu.SemaphoreType.DMA((4, 2)),
             pltpu.SemaphoreType.DMA((8, 2)),
-            pltpu.SemaphoreType.DMA((12, 2)),
         ],
         compiler_params=pltpu.CompilerParams(
             collective_id=0, has_side_effects=True, vmem_limit_bytes=58 * 1024 * 1024

time: 92.4 us -> 84.7 us (0.917)
  Pallas kernels: 90.3 us -> 83.2 us
    pallas_call x1, Pallas kernels: 90.3 us -> 83.2 us  [local(): pl.pallas_call(kernel, out_shape=jax.ShapeDtypeStruct((NK, 128), f32), in...]
where the time goes in v3:
time: 84.7 us; the launch traced here: 84.5 us
  Pallas kernels  83.2 us (98%)
  local copies, waits for them, and re-layouts  1.38 us (2%)
    pallas_call x1, Pallas kernels, local(): pl.pallas_call(kernel, out_shape=jax.ShapeDtypeStruct((NK, 128), f32), in...  83.2 us

profile of v3, /device:TPU:1, one launch (start us, length us, event | category | flops | bytes accessed | tf_op | source)
XLA Modules:
  0.0 84.5 jit_solution(9885795734218630341)
XLA Ops:
  0.0 83.2 %propagate.1 = f32[64,128]{1,0:T(8,128)} custom-call(f32[64,128]{1,0:T(8,128)} %rho_hbm.1, f32[64,2,8,1500]{3,2,1,0:T(8,128)} %bloch_hbm.1, f32[1500]{0:T(1024)} %coulomb_hbm.1, f32[8,64]{1,0:T(8,128)} %bitcast.3, f32[64,128]{1,0:T(8,128)} %dipole_hbm.1, s32[256]{0:T(256)} %count_hbm.1, s32[8,256]{1,0:T(8,128)} %bitcast.2, f32[256,512]{1,0:T(8,128)} %kernel_hbm.1, ...), custom_call_target="tpu_custom_call" | custom-call | tf_op jit(solution)/shard_map/propagate/pallas_call | solution.py:496
  83.2 1.4 %copy.12 = f32[64,128]{1,0:T(8,128)} copy(f32[64,128]{1,0:T(8,128)} %propagate.1) | data formatting | bytes 65536

commit v4 on v3

--- a/solution.py
+++ b/solution.py
@@ -162,29 +162,31 @@
 def build_pairs(bands, tail, pairs, first, last):
     top = iota((8, 128), 0) < 4
 
-    def build(k, _):
+    def build(step, _):
         edge = (TILES - 1) * 128
-        for part in range(2):
-            tail[k, part, :, : NG - edge] = bands[k, part, :, edge:]
-        for j in range(TILES):
-            lanes = slice(j * 128, (j + 1) * 128)
-            if j < TILES - 1:
-                u, v = bands[k, 0, :, lanes], bands[k, 1, :, lanes]
-            else:
-                u, v = tail[k, 0], tail[k, 1]
-            us = [u] + [rolled(u, d) for d in (1, 2, 3, 4)]
-            vs = [v] + [rolled(v, d) for d in (1, 2, 3, 4)]
-            values = [
-                u * u + v * v,
-                u * jnp.where(top, us[4], vs[4]) + v * jnp.where(top, vs[4], -us[4]),
-            ]
-            for d in (1, 2, 3):
-                values += [u * us[d] + v * vs[d], u * vs[d] - v * us[d]]
-            for t, value in enumerate(values):
-                pairs[j // HALF, k * 8 + t, :, (j % HALF) * 128 : (j % HALF + 1) * 128] = value
+        for k in (2 * step, 2 * step + 1):
+            for part in range(2):
+                tail[k, part, :, : NG - edge] = bands[k, part, :, edge:]
+        for k in (2 * step, 2 * step + 1):
+            for j in range(TILES):
+                lanes = slice(j * 128, (j + 1) * 128)
+                if j < TILES - 1:
+                    u, v = bands[k, 0, :, lanes], bands[k, 1, :, lanes]
+                else:
+                    u, v = tail[k, 0], tail[k, 1]
+                us = [u] + [rolled(u, d) for d in (1, 2, 3, 4)]
+                vs = [v] + [rolled(v, d) for d in (1, 2, 3, 4)]
+                values = [
+                    u * u + v * v,
+                    u * jnp.where(top, us[4], vs[4]) + v * jnp.where(top, vs[4], -us[4]),
+                ]
+                for d in (1, 2, 3):
+                    values += [u * us[d] + v * vs[d], u * vs[d] - v * us[d]]
+                for t, value in enumerate(values):
+                    pairs[j // HALF, k * 8 + t, :, (j % HALF) * 128 : (j % HALF + 1) * 128] = value
         return 0
 
-    lax.fori_loop(first, last, build, 0)
+    lax.fori_loop(first // 2, last // 2, build, 0)
 
 
 def loop(body, carry):
@@ -493,6 +495,7 @@
 def local(delta_rho, bloch_blocks, coulomb, energies, dipole, pair_count, pair_target, kernel_list):
     into, back = component_tables()
     hbm = pl.BlockSpec(memory_space=pltpu.HBM)
+    pin = functools.partial(pltpu.with_memory_space_constraint, memory_space=pltpu.HBM)
     return pl.pallas_call(
         kernel,
         out_shape=jax.ShapeDtypeStruct((NK, 128), f32),
@@ -528,20 +531,17 @@
             pltpu.SemaphoreType.DMA((8, 2)),
         ],
         compiler_params=pltpu.CompilerParams(
-            collective_id=0, has_side_effects=True, vmem_limit_bytes=58 * 1024 * 1024
+            collective_id=0, has_side_effects=True, vmem_limit_bytes=44 * 1024 * 1024
         ),
         name="propagate",
     )(
-        delta_rho,
-        bloch_blocks,
-        coulomb,
-        energies.T,
-        dipole,
-        pair_count,
-        pair_target.T,
-        kernel_list,
-        jnp.asarray(into),
-        jnp.asarray(back),
+        *[
+            pin(value)
+            for value in (
+                delta_rho, bloch_blocks, coulomb, energies.T, dipole, pair_count, pair_target.T, kernel_list,
+                jnp.asarray(into), jnp.asarray(back),
+            )
+        ],
     )
 
 

time: 84.7 us -> 83.2 us (0.982)
  no operation moved by 1% of the time
where the time goes in v4:
time: 83.2 us; the launch traced here: 83.1 us
  Pallas kernels  82.4 us (99%)
    pallas_call x1, Pallas kernels, local(): pl.pallas_call(kernel, out_shape=jax.ShapeDtypeStruct((NK, 128), f32), in...  82.4 us

profile of v4, /device:TPU:1, one launch (start us, length us, event | category | flops | bytes accessed | tf_op | source)
XLA Modules:
  0.0 83.1 jit_solution(7048730539560920210)
XLA Ops:
  0.0 82.4 %propagate.1 = f32[64,128]{1,0:T(8,128)S(1)} custom-call(f32[64,128]{1,0:T(8,128)} %rho_hbm.1, f32[64,2,8,1500]{3,2,1,0:T(8,128)} %bloch_hbm.1, f32[1500]{0:T(1024)} %coulomb_hbm.1, f32[8,64]{1,0:T(8,128)} %bitcast.3, f32[64,128]{1,0:T(8,128)} %dipole_hbm.1, s32[256]{0:T(256)} %count_hbm.1, s32[8,256]{1,0:T(8,128)} %bitcast.2, f32[256,512]{1,0:T(8,128)} %kernel_hbm.1, ...), custom_call_target="tpu_custom_call" | custom-call | tf_op jit(solution)/shard_map/propagate/pallas_call | solution.py:499
  82.4 0.6 copy.12

commit v5 on v4

--- a/solution.py
+++ b/solution.py
@@ -325,11 +325,6 @@
     blocks = iota((8, 256), 1)
     counts = jnp.broadcast_to(count_buf[...].reshape(1, 256), (8, 256))
     live = iota((8, 256), 0) < counts
-    wide_row = iota((256, 256), 0)
-    wide_lane = iota((256, 256), 1)
-    same = wide_row // 8 == wide_lane // 8
-    before = same & (wide_row < wide_lane)
-    lower = iota((8, 8), 1) < iota((8, 8), 0)
 
     own_block = (iota((256, 128), 0) == ka * 8 + lax.rem(iota((256, 128), 1), 8)) & (iota((256, 128), 1) < 64)
     on_p = row == lane // 8
@@ -360,24 +355,6 @@
         spread_rows = exact(entry_rows, pick, 1, 0)
         keep = (lax.rem(square_row, 8) == square_lane // 8) & (square_lane < 64)
         couple[part] = -exact(hot, jnp.where(keep, spread_rows, 0.0), 1, 0)
-
-    mine = live & (target // 8 == ka)
-    mine_f = mine.astype(f32)
-    ranks = exact(mine, before, 1, 0) + exact(exact(lower, mine, 1, 0), same, 1, 0)
-    source = wide_lane // 8
-    source_device = (
-        lax.rem(chip_x + SIDE - source // 8, SIDE) * SIDE + lax.rem(chip_z + SIDE - lax.rem(source // 2, SIDE), SIDE)
-    ) * 2 + lax.rem(core + lax.rem(source, 2), 2)
-    placed = jnp.zeros((8, 256), f32)
-    for number in range(2):
-        of_slot = jnp.where(ranks == number, mine_f, 0.0)
-        by_block = jnp.zeros((8, 256), f32)
-        for q in range(8):
-            found = jnp.sum(jnp.where(lax.rem(target, 8) == q, of_slot, 0.0), axis=0, keepdims=True)
-            by_block = jnp.where(iota((8, 256), 0) == q, found, by_block)
-        into_column = (wide_row // 8 == source_device) & (lax.rem(wide_lane, 8) == HALF + number)
-        placed = placed + exact(by_block, into_column, 1, 0)
-    place[...] = placed
 
     for n, copy in enumerate(band_loads):
         copy.wait()
@@ -421,6 +398,33 @@
                 second_send.at[par], second_recv.at[par, n], send_sem.at[1, par], recv_sem.at[1, par], layer_ids[n]
             ).start()
         second_recv[par, 0] = second_send[par]
+
+        @pl.when(e == 0)
+        def _():
+            target = target_buf[...]
+            counts = jnp.broadcast_to(count_buf[...].reshape(1, 256), (8, 256))
+            wide_row = iota((256, 256), 0)
+            wide_lane = iota((256, 256), 1)
+            same = wide_row // 8 == wide_lane // 8
+            before = same & (wide_row < wide_lane)
+            lower = iota((8, 8), 1) < iota((8, 8), 0)
+            mine = (iota((8, 256), 0) < counts) & (target // 8 == ka)
+            mine_f = mine.astype(f32)
+            ranks = exact(mine, before, 1, 0) + exact(exact(lower, mine, 1, 0), same, 1, 0)
+            source = wide_lane // 8
+            source_device = (
+                lax.rem(chip_x + SIDE - source // 8, SIDE) * SIDE + lax.rem(chip_z + SIDE - lax.rem(source // 2, SIDE), SIDE)
+            ) * 2 + lax.rem(core + lax.rem(source, 2), 2)
+            placed = jnp.zeros((8, 256), f32)
+            for number in range(2):
+                of_slot = jnp.where(ranks == number, mine_f, 0.0)
+                by_block = jnp.zeros((8, 256), f32)
+                for q in range(8):
+                    found = jnp.sum(jnp.where(lax.rem(target, 8) == q, of_slot, 0.0), axis=0, keepdims=True)
+                    by_block = jnp.where(iota((8, 256), 0) == q, found, by_block)
+                into_column = (wide_row // 8 == source_device) & (lax.rem(wide_lane, 8) == HALF + number)
+                placed = placed + exact(by_block, into_column, 1, 0)
+            place[...] = placed
 
         def total_of(parts):
             while len(parts) > 1:

time: 83.2 us -> 82.4 us (level)
  no operation moved by 1% of the time
where the time goes in v5:
time: 82.4 us; the launch traced here: 82.3 us
  Pallas kernels  81.7 us (99%)
    pallas_call x1, Pallas kernels, local(): pl.pallas_call(kernel, out_shape=jax.ShapeDtypeStruct((NK, 128), f32), in...  81.7 us

profile of v5, /device:TPU:1, one launch (start us, length us, event | category | flops | bytes accessed | tf_op | source)
XLA Modules:
  0.0 82.3 jit_solution(10899299485031259362)
XLA Ops:
  0.0 81.7 %propagate.1 = f32[64,128]{1,0:T(8,128)S(1)} custom-call(f32[64,128]{1,0:T(8,128)} %rho_hbm.1, f32[64,2,8,1500]{3,2,1,0:T(8,128)} %bloch_hbm.1, f32[1500]{0:T(1024)} %coulomb_hbm.1, f32[8,64]{1,0:T(8,128)} %bitcast.3, f32[64,128]{1,0:T(8,128)} %dipole_hbm.1, s32[256]{0:T(256)} %count_hbm.1, s32[8,256]{1,0:T(8,128)} %bitcast.2, f32[256,512]{1,0:T(8,128)} %kernel_hbm.1, ...), custom_call_target="tpu_custom_call" | custom-call | tf_op jit(solution)/shard_map/propagate/pallas_call | solution.py:503
  81.7 0.6 copy.12
